TPU v7x, 32 devices: a whole 2x2x4 slice. The times are simulated.
32 devices in a mesh: tr: 4 (over x, core), gz: 8 (over z, y).
Axes of the slice: x: 2, y: 2, z: 4, core: 2. Of those that a mesh axis runs over, the one named last changes fastest.
Arguments:
- tokens: bfloat16 [40, 32, 8, 768], P('gz', None, 'tr'), may hold values from -6 to 6
- cotangent: bfloat16 [40, 32, 8, 768], P('gz', None, 'tr'), may hold values from -6 to 6
- gain_x: float32 [768], replicated, may hold values from 0.1 to 1.9
- wqkv_x: bfloat16 [768, 2304], P('tr'), as said below
- wo_x: bfloat16 [768, 768], P('tr'), may hold values from -0.21875 to 0.21875
- gain_z: float32 [768], replicated, may hold values from 0.1 to 1.9
- wqkv_z: bfloat16 [768, 2304], P('tr'), as said below
- wo_z: bfloat16 [768, 768], P('tr'), may hold values from -0.21875 to 0.21875
Outputs:
- grad_tokens: bfloat16 [40, 32, 8, 768], P('gz', None, 'tr')
Inputs may be any that keep to these rules, and one draw needn't show every extreme that they name: `wqkv_x`: query, key and value columns side by side, each block split into 6 heads of 128. `wqkv_z`: query, key and value columns side by side, each block split into 6 heads of 128.
All inputs are finite; a program needn't handle non-finite values.
Results may differ from a plain program's by a relative error of at most 0.038.
The roundings to bfloat16 on the way count: a program that leaves them out, or rounds other values in their place, can miss the bound.
Values may be sent and summed in bfloat16 or wider, within the bound.
A program may use at most 64 MiB of HBM per device.

v0:
```python
import functools
import math

import jax
import jax.numpy as jnp
import numpy as np
from jax import lax
from jax.experimental import pallas as pl
from jax.experimental.pallas import tpu as pltpu
from jax.sharding import PartitionSpec as P

H = 6


def head_split(packed, index, model_width):
    piece = packed[..., index * model_width : (index + 1) * model_width]
    return piece.reshape(piece.shape[:-1] + (H, model_width // H))


def merge_heads(value):
    return value.reshape(value.shape[:-2] + (value.shape[-2] * value.shape[-1],))


def recompute(tokens_in, gain_vec, w_in, layout):
    model_width = w_in.shape[0]
    factor = 1.0 / math.sqrt(model_width // H)
    widened = tokens_in.astype(jnp.float32)
    inv_rms = lax.rsqrt(jnp.mean(widened * widened, axis=-1, keepdims=True) + 1e-06)
    normed = (widened * inv_rms * gain_vec).astype(jnp.bfloat16)
    packed = jnp.dot(normed, w_in, preferred_element_type=jnp.float32).astype(jnp.bfloat16)
    queries = head_split(packed, 0, model_width)
    key_part = head_split(packed, 1, model_width)
    values = head_split(packed, 2, model_width)
    key_form = layout.replace("l", "m")
    scores = (
        jnp.einsum(
            layout + "," + key_form + "->bhlm",
            queries,
            key_part,
            preferred_element_type=jnp.float32,
        )
        * factor
    )
    highest = jnp.max(scores, axis=-1, keepdims=True)
    expanded = jnp.exp(scores - highest)
    probs = expanded / jnp.sum(expanded, axis=-1, keepdims=True)
    return (widened, inv_rms, queries, key_part, values, probs, probs.astype(jnp.bfloat16), factor)


def forward_out(tokens_in, gain_vec, w_in, w_out, layout):
    widened, inv_rms, queries, key_part, values, probs, probs_b, factor = recompute(
        tokens_in, gain_vec, w_in, layout
    )
    key_form = layout.replace("l", "m")
    mixed = jnp.einsum(
        "bhlm," + key_form + "->" + layout, probs_b, values, preferred_element_type=jnp.float32
    )
    mixed = merge_heads(mixed.astype(jnp.bfloat16))
    return (widened + jnp.dot(mixed, w_out, preferred_element_type=jnp.float32)).astype(
        jnp.bfloat16
    )


def backward(tokens_in, upstream, gain_vec, w_in, w_out, layout):
    widened, inv_rms, queries, key_part, values, probs, probs_b, factor = recompute(
        tokens_in, gain_vec, w_in, layout
    )
    key_form = layout.replace("l", "m")
    d_mixed = jnp.dot(upstream, w_out.T, preferred_element_type=jnp.float32).astype(jnp.bfloat16)
    d_mixed = d_mixed.reshape(d_mixed.shape[:-1] + (H, d_mixed.shape[-1] // H))
    d_probs = jnp.einsum(
        layout + "," + key_form + "->bhlm", d_mixed, values, preferred_element_type=jnp.float32
    )
    d_values = jnp.einsum(
        "bhlm," + layout + "->" + key_form, probs_b, d_mixed, preferred_element_type=jnp.float32
    ).astype(jnp.bfloat16)
    centre = jnp.sum(probs * d_probs, axis=-1, keepdims=True)
    d_scores = (probs * (d_probs - centre) * factor).astype(jnp.bfloat16)
    d_queries = jnp.einsum(
        "bhlm," + key_form + "->" + layout, d_scores, key_part, preferred_element_type=jnp.float32
    ).astype(jnp.bfloat16)
    d_keys = jnp.einsum(
        "bhlm," + layout + "->" + key_form, d_scores, queries, preferred_element_type=jnp.float32
    ).astype(jnp.bfloat16)
    joined = jnp.concatenate(
        [merge_heads(d_queries), merge_heads(d_keys), merge_heads(d_values)], axis=-1
    )
    d_normed = jnp.dot(joined, w_in.T, preferred_element_type=jnp.float32)
    scaled = d_normed * gain_vec
    d_tokens = inv_rms * (
        scaled - widened * inv_rms * inv_rms * jnp.mean(scaled * widened, axis=-1, keepdims=True)
    )
    return (upstream.astype(jnp.float32) + d_tokens).astype(jnp.bfloat16)


def line_forward(lines, gain_vec, w_in, w_out):
    feature_count = lines.shape[3]
    flat = lines.reshape(-1, lines.shape[2], feature_count)
    return forward_out(flat, gain_vec, w_in, w_out, "blhe").reshape(lines.shape)


def line_backward(lines, upstream, gain_vec, w_in, w_out):
    feature_count = lines.shape[3]
    flat = lines.reshape(-1, lines.shape[2], feature_count)
    flat_up = upstream.reshape(flat.shape)
    return backward(flat, flat_up, gain_vec, w_in, w_out, "blhe").reshape(lines.shape)


def per_device(tokens, cotangent, gain_x, wqkv_x, wo_x, gain_z, wqkv_z, wo_z):
    full_in_x, full_out_x = (
        lax.all_gather(wqkv_x, "tr", axis=0, tiled=True),
        lax.all_gather(wo_x, "tr", axis=0, tiled=True),
    )
    full_in_z, full_out_z = (
        lax.all_gather(wqkv_z, "tr", axis=0, tiled=True),
        lax.all_gather(wo_z, "tr", axis=0, tiled=True),
    )
    width = tokens.shape[-1]
    lines = lax.all_to_all(tokens, "tr", split_axis=1, concat_axis=2, tiled=True)
    cot_lines = lax.all_to_all(cotangent, "tr", split_axis=1, concat_axis=2, tiled=True)
    cells = lines.shape[1] * lines.shape[2]
    flat = (lines.shape[0], cells, width)
    cot_columns = lax.all_to_all(
        cot_lines.reshape(flat), "gz", split_axis=1, concat_axis=0, tiled=True
    )
    mid_lines = line_forward(lines, gain_x, full_in_x, full_out_x)
    mid_columns = lax.all_to_all(
        mid_lines.reshape(flat), "gz", split_axis=1, concat_axis=0, tiled=True
    )
    grad_columns = backward(
        mid_columns, cot_columns, gain_z, full_in_z, full_out_z, "lbhe"
    )
    grad_lines = lax.all_to_all(grad_columns, "gz", split_axis=0, concat_axis=1, tiled=True)
    result_lines = line_backward(lines, grad_lines.reshape(lines.shape), gain_x, full_in_x, full_out_x)
    return lax.all_to_all(result_lines, "tr", split_axis=2, concat_axis=1, tiled=True)


F32, BF16 = jnp.float32, jnp.bfloat16


def nt(a, b):
    return lax.dot_general(a, b, (((1,), (1,)), ((), ())), preferred_element_type=F32)


def tn(a, b):
    return lax.dot_general(a, b, (((0,), (0,)), ((), ())), preferred_element_type=F32)


def nn(a, b):
    return jnp.dot(a, b, preferred_element_type=F32)


def flat(value):
    width = value.shape[-1]
    return value.astype(F32).reshape(-1, width)


def project(a, gain, w, qkv):
    rows, width = a.shape
    rstd = lax.rsqrt(jnp.mean(a * a, axis=-1, keepdims=True) + 1e-06)
    normed = (a * rstd * gain).astype(BF16)

    def part(j, _):
        cols = pl.ds(pl.multiple_of(j * width, width), width)
        qkv[:, cols] = nn(normed, w[:, cols]).astype(BF16)
        return 0

    lax.fori_loop(0, 3, part, 0)
    return rstd


def line_mask(block, line):
    key = lax.broadcasted_iota(jnp.int32, (block, block), 0) // line
    query = lax.broadcasted_iota(jnp.int32, (block, block), 1) // line
    return key == query


def attend_forward(qkv, probs, mixed, block, line):
    rows, width = mixed.shape
    size = width // H
    mask = line_mask(block, line)
    factor = 1.0 / math.sqrt(size)

    def body(b, _):
        at = pl.ds(pl.multiple_of(b * block, block), block)
        for first in range(0, H, 6):
            heads = range(first, first + 6)
            spans = [[pl.ds(n * width + h * size, size) for n in range(3)] for h in heads]
            qk = [nt(qkv[at, sp[1]], qkv[at, sp[0]]) for sp in spans]
            scores = [jnp.where(mask, x * factor, -1e30) for x in qk]
            tops = [jnp.max(x, axis=0, keepdims=True) for x in scores]
            grown = [jnp.exp(x - t) for x, t in zip(scores, tops)]
            sums = [1.0 / jnp.sum(x, axis=0, keepdims=True) for x in grown]
            ps = [x * t for x, t in zip(grown, sums)]
            for h, p in zip(heads, ps):
                probs[b * H + h] = p
            outs = [tn(p.astype(BF16), qkv[at, sp[2]]) for p, sp in zip(ps, spans)]
            for sp, o in zip(spans, outs):
                mixed[at, sp[0]] = o.astype(BF16)
        return 0

    lax.fori_loop(0, rows // block, body, 0, unroll=True)


def attend_backward(qkv, probs, d_mixed, joined, block, line, keep):
    rows, width = d_mixed.shape
    size = width // H
    mask = line_mask(block, line)
    factor = 1.0 / math.sqrt(size)

    def body(b, _):
        at = pl.ds(pl.multiple_of(b * block, block), block)
        for first in range(0, H, 6):
            heads = range(first, first + 6)
            spans = [[pl.ds(n * width + h * size, size) for n in range(3)] for h in heads]
            dps = [nt(qkv[at, sp[2]], d_mixed[at, sp[0]]) for sp in spans]
            if keep:
                ps = [probs[b * H + h] for h in heads]
            else:
                qk = [nt(qkv[at, sp[1]], qkv[at, sp[0]]) for sp in spans]
                scores = [jnp.where(mask, x * factor, -1e30) for x in qk]
                tops = [jnp.max(x, axis=0, keepdims=True) for x in scores]
                grown = [jnp.exp(x - t) for x, t in zip(scores, tops)]
                sums = [1.0 / jnp.sum(x, axis=0, keepdims=True) for x in grown]
                ps = [x * t for x, t in zip(grown, sums)]
            dvs = [nn(p.astype(BF16), d_mixed[at, sp[0]]) for p, sp in zip(ps, spans)]
            centres = [jnp.sum(p * dp, axis=0, keepdims=True) for p, dp in zip(ps, dps)]
            dss = [
                (p * (dp - c) * factor).astype(BF16) for p, dp, c in zip(ps, dps, centres)
            ]
            dks = [nn(ds, qkv[at, sp[0]]) for ds, sp in zip(dss, spans)]
            dqs = [tn(ds, qkv[at, sp[1]]) for ds, sp in zip(dss, spans)]
            for sp, dq, dk, dv in zip(spans, dqs, dks, dvs):
                joined[at, sp[0]] = dq.astype(BF16)
                joined[at, sp[1]] = dk.astype(BF16)
                joined[at, sp[2]] = dv.astype(BF16)
        return 0

    lax.fori_loop(0, rows // block, body, 0, unroll=True)


def norm_backward(a, c, rstd, gain, joined, w, dn):
    width = a.shape[-1]
    for j in range(3):
        part = width // 3
        dn[:, j * part : (j + 1) * part] = nt(joined[...], w[j * part : (j + 1) * part, :])
    scaled = dn[...] * gain
    mean = jnp.mean(scaled * a, axis=-1, keepdims=True)
    return (c + rstd * (scaled - a * (rstd * rstd) * mean)).astype(BF16)


def kernel(
    nt_, ng, block_x, line_x, block_z, line_z,
    tok, cot, gain_x, wx, ox, gain_z, wz, oz, px, pz, out,
    tokr, cotr, outs, outr, mids, midr, cots, cotz, grads, gradr,
    fwx, fox, fwz, foz, qkvx, qkvz, probs, mixed, dmix, joined, dn, ax, az,
    tr_send, tr_recv, gz_send, gz_recv, w_send, w_recv, local,
):
    me, mine = lax.axis_index("tr"), lax.axis_index("gz")
    sib, across = me + 1 - 2 * (me % 2), (me + 2) % nt_
    half = mine % 2
    partner = mine + 1 - 2 * half
    rows, width = ax.shape

    barrier = pltpu.get_barrier_semaphore()
    for d in range(1, nt_):
        pl.semaphore_signal(barrier, inc=1, device_id=((me + d) % nt_, mine), device_id_type=pl.DeviceIdType.MESH)
    for d in range(1, ng):
        pl.semaphore_signal(barrier, inc=1, device_id=(me, (mine + d) % ng), device_id_type=pl.DeviceIdType.MESH)
    pl.semaphore_wait(barrier, nt_ + ng - 2)

    def remote(src, dst, send, recv, t, g):
        return pltpu.make_async_remote_copy(
            src_ref=src, dst_ref=dst, send_sem=send, recv_sem=recv,
            device_id=(t, g), device_id_type=pl.DeviceIdType.MESH,
        )

    def tr_copy(n, source, slots, d):
        t = (me + d) % nt_
        return remote(source(t), slots.at[me], tr_send.at[n, d], tr_recv.at[n, d], t, mine)

    def gz_copy(n, source, slots, d):
        g = (mine + d) % ng
        return remote(source.at[g], slots.at[mine], gz_send.at[n, d], gz_recv.at[n, d], me, g)

    far_first = [2, 3, 1] if nt_ == 4 else list(range(1, nt_))
    gz_order = sorted(range(1, ng), key=lambda d: -min(d, ng - d))

    owns = ((wx, wx, wx, ox), (wz, wz, wz, oz))
    fulls = ((fwx, fwx, fwx, fox), (fwz, fwz, fwz, foz))

    def piece(ref, k, t, h, mine_only):
        depth = ref.shape[0] if mine_only else ref.shape[0] // nt_
        cols = width // 2
        first = h * 3 + k if k < 3 else h
        col = pl.ds(pl.multiple_of(first * cols, 128), cols)
        row = pl.ds(0, depth) if mine_only else pl.ds(pl.multiple_of(t * depth, 16), depth)
        return ref.at[row, col]

    def own_copy(s, k, n, h, t):
        return remote(
            piece(owns[s][k], k, me, h, True), piece(fulls[s][k], k, me, h, False),
            w_send.at[s, k, n], w_recv.at[s, k, me, h], t, mine,
        )

    def relay(s, k, n, h, t, g):
        spot = piece(fulls[s][k], k, across, h, False)
        return remote(spot, spot, w_send.at[s, k, n], w_recv.at[s, k, across, h], t, g)

    def arrive(s, k, src, h):
        spot = piece(fulls[s][k], k, src, h, False)
        remote(spot, spot, w_send.at[s, k, 0], w_recv.at[s, k, src, h], sib, mine).wait_recv()

    def weights_begin(s):
        for k in range(4):
            own_copy(s, k, 2, half, across).start()
        for k in range(4):
            own_copy(s, k, 0, 0, sib).start()
            own_copy(s, k, 1, 1, sib).start()

    def weights_relay(s, pieces=range(4)):
        for k in pieces:
            arrive(s, k, across, half)
            relay(s, k, 3, half, me, partner).start()
            relay(s, k, 4, half, sib, mine).start()

    def weights_end(s):
        far = (sib + 2) % nt_
        for k in range(4):
            arrive(s, k, across, 1 - half)
            relay(s, k, 5, 1 - half, sib, mine).start()
        for k in range(4):
            for h in range(2):
                arrive(s, k, sib, h)
                arrive(s, k, far, h)
            own_copy(s, k, 0, 0, sib).wait_send()
            own_copy(s, k, 1, 1, sib).wait_send()
            own_copy(s, k, 2, half, across).wait_send()
            relay(s, k, 3, half, me, partner).wait_send()
            relay(s, k, 4, half, sib, mine).wait_send()
            relay(s, k, 5, 1 - half, sib, mine).wait_send()

    def wait_tr(n, source, slots):
        for d in range(1, nt_):
            tr_copy(n, source, slots, d).wait_send()
            src = (me + nt_ - d) % nt_
            remote(source(src), slots.at[src], tr_send.at[n, d], tr_recv.at[n, d], src, mine).wait_recv()

    def wait_gz(n, source, slots):
        for d in range(1, ng):
            gz_copy(n, source, slots, d).wait_send()
            src = (mine + ng - d) % ng
            remote(source.at[src], slots.at[src], gz_send.at[n, d], gz_recv.at[n, d], me, src).wait_recv()

    def from_tok(t):
        return tok.at[:, t]

    def from_cot(t):
        return cot.at[:, t]

    def from_out(t):
        return outs.at[t]

    for d in far_first:
        tr_copy(0, from_tok, tokr, d).start()
    weights_begin(0)
    for d in far_first:
        tr_copy(1, from_cot, cotr, d).start()
    here = [pltpu.make_async_copy(tok.at[:, me], tokr.at[me], local.at[0]),
            pltpu.make_async_copy(cot.at[:, me], cotr.at[me], local.at[1])]
    n = 2
    for s in range(2):
        for k in (0, 3):
            depth = owns[s][k].shape[0]
            to = fulls[s][k].at[pl.ds(pl.multiple_of(me * depth, 16), depth)]
            here.append(pltpu.make_async_copy(owns[s][k], to, local.at[n]))
            n += 1
    for copy in here:
        copy.start()
    for copy in here:
        copy.wait()
    wait_tr(0, from_tok, tokr)
    ax[...] = nn(px[...], flat(tokr[...]).astype(BF16)).astype(BF16)

    weights_relay(0)
    weights_begin(1)
    wait_tr(1, from_cot, cotr)
    cot_lines = nn(px[...], flat(cotr[...]).astype(BF16))
    cots[...] = cot_lines.reshape(cots.shape).astype(BF16)
    cotz[mine] = cots[mine]
    for d in gz_order:
        gz_copy(1, cots, cotz, d).start()
    weights_end(0)

    rstd_x = project(ax[...].astype(F32), gain_x[...][None], fwx, qkvx)
    weights_relay(1, (0, 1))
    attend_forward(qkvx, probs, mixed, block_x, line_x)
    weights_relay(1, (2, 3))
    mid = ax[...].astype(F32) + nn(mixed[...], fox[...])
    mids[...] = mid.reshape(mids.shape).astype(BF16)
    for d in gz_order:
        gz_copy(0, mids, midr, d).start()
    midr[mine] = mids[mine]
    weights_end(1)

    wait_gz(1, cots, cotz)
    cz = nn(pz[...], flat(cotz[...]).astype(BF16))
    dmix[...] = nt(cz.astype(BF16), foz[...]).astype(BF16)
    wait_gz(0, mids, midr)
    az[...] = nn(pz[...], flat(midr[...]).astype(BF16)).astype(BF16)
    rstd_z = project(az[...].astype(F32), gain_z[...][None], fwz, qkvz)
    attend_backward(qkvz, probs, dmix, joined, block_z, line_z, False)
    cz = nn(pz[...], flat(cotz[...]).astype(BF16))
    back = norm_backward(az[...].astype(F32), cz, rstd_z, gain_z[...][None], joined, fwz, dn)
    grads[...] = tn(pz[...], back).reshape(grads.shape).astype(BF16)
    for d in gz_order:
        gz_copy(2, grads, gradr, d).start()
    gradr[mine] = grads[mine]
    wait_gz(2, grads, gradr)

    dmix[...] = nt(flat(gradr[...]).astype(BF16), fox[...]).astype(BF16)
    attend_backward(qkvx, probs, dmix, joined, block_x, line_x, True)
    back = norm_backward(
        ax[...].astype(F32), flat(gradr[...]), rstd_x, gain_x[...][None], joined, fwx, dn
    )
    outs[...] = tn(px[...], back).reshape(outs.shape).astype(BF16)
    for d in far_first:
        tr_copy(2, from_out, outr, d).start()
    outr[me] = outs[me]
    wait_tr(2, from_out, outr)
    for t in range(nt_):
        out[:, t] = outr[t]


def one_hot(order):
    return jnp.asarray(np.eye(len(order), dtype=np.float32)[order], BF16)


def fits_kernel(trs, gzs, slab, y, x_own, width):
    rows_own = y // trs
    return trs == 4 and rows_own == gzs and (slab * trs * x_own) % 8 == 0 and (rows_own * x_own) % 16 == 0


def fused(trs, gzs, tokens, cotangent, gain_x, wqkv_x, wo_x, gain_z, wqkv_z, wo_z):
    slab, y, x_own, width = tokens.shape
    y_own, x = y // trs, x_own * trs
    rows, z = slab * y * x_own, slab * gzs
    share = rows // gzs
    index = np.arange(rows).reshape(trs, slab, y_own, x_own)
    px = one_hot(index.transpose(2, 1, 0, 3).reshape(-1))
    pz = one_hot(np.arange(rows).reshape(z, x).T.reshape(-1))
    split = (slab, trs, y_own * x_own, width)
    block_x, block_z = 80 if 80 % x == 0 else x, 80 if 80 % z == 0 else z
    tr_slots, gz_slots = (trs, slab, y_own * x_own, width), (gzs, share, width)
    vm = pl.BlockSpec(memory_space=pltpu.VMEM)
    hbm = pl.BlockSpec(memory_space=pl.ANY)
    wide = wqkv_x.shape[1]
    result = pl.pallas_call(
        functools.partial(kernel, trs, gzs, block_x, x, block_z, z),
        out_shape=jax.ShapeDtypeStruct(split, BF16),
        in_specs=[hbm, hbm, vm, hbm, hbm, vm, hbm, hbm, vm, vm],
        out_specs=vm,
        scratch_shapes=[pltpu.VMEM(tr_slots, BF16)] * 4
        + [pltpu.VMEM(gz_slots, BF16)] * 6
        + [pltpu.VMEM((width, wide), BF16), pltpu.VMEM((width, width), BF16)] * 2
        + [pltpu.VMEM((rows, wide), BF16)] * 2
        + [pltpu.VMEM((rows // block_x * H, block_x, block_x), F32)]
        + [pltpu.VMEM((rows, width), BF16)] * 2
        + [pltpu.VMEM((rows, wide), BF16), pltpu.VMEM((rows, width), F32)]
        + [pltpu.VMEM((rows, width), BF16)] * 2
        + [
            pltpu.SemaphoreType.DMA((3, trs)),
            pltpu.SemaphoreType.DMA((3, trs)),
            pltpu.SemaphoreType.DMA((3, gzs)),
            pltpu.SemaphoreType.DMA((3, gzs)),
            pltpu.SemaphoreType.DMA((2, 4, 6)),
            pltpu.SemaphoreType.DMA((2, 4, trs, 2)),
            pltpu.SemaphoreType.DMA((6,)),
        ],
        compiler_params=pltpu.CompilerParams(
            collective_id=0, has_side_effects=True, vmem_limit_bytes=56 * 1024 * 1024
        ),
    )(
        tokens.reshape(split), cotangent.reshape(split),
        gain_x, wqkv_x, wo_x, gain_z, wqkv_z, wo_z, px, pz,
    )
    return result.reshape(tokens.shape)


def solution(mesh):
    trs, gzs = mesh.shape["tr"], mesh.shape["gz"]

    def body(tokens, *rest):
        if fits_kernel(trs, gzs, *tokens.shape):
            return fused(trs, gzs, tokens, *rest)
        return per_device(tokens, *rest)

    return jax.shard_map(
        body,
        mesh=mesh,
        in_specs=(
            P("gz", None, "tr", None),
            P("gz", None, "tr", None),
            P(),
            P("tr", None),
            P("tr", None),
            P(),
            P("tr", None),
            P("tr", None),
        ),
        out_specs=P("gz", None, "tr", None),
        check_vma=False,
    )
```

profile of v0, /device:TPU:0, one launch (start us, length us, event | category | flops | bytes accessed | tf_op | source)
XLA Modules:
  0.0 95.2 jit_solution(3962409831156448853)
XLA Ops:
  0.0 0.0 copy-start
  0.0 2.0 %reshape.9.tok = bf16[5,4,16,768]{3,2,1,0:T(8,128)(2,1)} reshape(bf16[5,32,2,768]{3,2,1,0:T(2,128)(2,1)} %param.10) | data formatting | bytes 983040 | tf_op jit(solution)/shard_map/reshape | solution.py:484
  2.1 0.0 copy-done
  2.1 1.0 %reshape.10.cot = bf16[5,4,16,768]{3,2,1,0:T(8,128)(2,1)} reshape(bf16[5,32,2,768]{3,2,1,0:T(2,128)(2,1)S(1)} %copy-done) | data formatting | bytes 983040 | tf_op jit(solution)/shard_map/reshape | solution.py:484
  3.0 90.1 %shard_map.100 = bf16[5,4,16,768]{3,2,1,0:T(8,128)(2,1)} custom-call(bf16[5,4,16,768]{3,2,1,0:T(8,128)(2,1)} %reshape.9.tok, bf16[5,4,16,768]{3,2,1,0:T(8,128)(2,1)} %reshape.10.cot, f32[768]{0:T(1024)} %gain_x.1, bf16[192,2304]{1,0:T(8,128)(2,1)} %wx.1, bf16[192,768]{1,0:T(8,128)(2,1)} %ox.1, f32[768]{0:T(1024)} %gain_z.1, bf16[192,2304]{1,0:T(8,128)(2,1)} %wz.1, ...), custom_call_target="tpu_custom_call" | custom-call | tf_op jit(solution)/shard_map/pallas_call | solution.py:458
  93.2 2.0 %reshape.11 = bf16[5,32,2,768]{3,2,1,0:T(2,128)(2,1)} reshape(bf16[5,4,16,768]{3,2,1,0:T(8,128)(2,1)} %shard_map.100) | data formatting | bytes 983040 | tf_op jit(solution)/shard_map/reshape | solution.py:487
Async XLA Ops:
  0.0 2.1 %copy-start = (bf16[5,32,2,768]{3,2,1,0:T(2,128)(2,1)S(1)}, bf16[5,32,2,768]{3,2,1,0:T(2,128)(2,1)}, u32[]{:S(2)}) copy-start(bf16[5,32,2,768]{3,2,1,0:T(2,128)(2,1)} %param.11) | copy-start | bytes 1474564
where the time goes:
time: 96 us; the launch traced here: 95.2 us
  Pallas kernels  90.1 us (94%)
  local copies, waits for them, and re-layouts  5.01 us (5%)
    pallas_call x1, Pallas kernels, fused(): pl.pallas_call(functools.partial(kernel, trs, gzs, block_x, x, block_z, z...  90.1 us
    reshape x1, local copies, waits for them, and re-layouts, fused(): tokens.reshape(split)  2.05 us
    reshape x1, local copies, waits for them, and re-layouts, fused(): return result.reshape(tokens.shape)  1.99 us

commit v1 on v0

v1 whole, which is shorter than its diff:
```python
import functools
import math

import jax
import jax.numpy as jnp
import numpy as np
from jax import lax
from jax.experimental import pallas as pl
from jax.experimental.pallas import tpu as pltpu
from jax.sharding import PartitionSpec as P

H = 6


def head_split(packed, index, model_width):
    piece = packed[..., index * model_width : (index + 1) * model_width]
    return piece.reshape(piece.shape[:-1] + (H, model_width // H))


def merge_heads(value):
    return value.reshape(value.shape[:-2] + (value.shape[-2] * value.shape[-1],))


def recompute(tokens_in, gain_vec, w_in, layout):
    model_width = w_in.shape[0]
    factor = 1.0 / math.sqrt(model_width // H)
    widened = tokens_in.astype(jnp.float32)
    inv_rms = lax.rsqrt(jnp.mean(widened * widened, axis=-1, keepdims=True) + 1e-06)
    normed = (widened * inv_rms * gain_vec).astype(jnp.bfloat16)
    packed = jnp.dot(normed, w_in, preferred_element_type=jnp.float32).astype(jnp.bfloat16)
    queries = head_split(packed, 0, model_width)
    key_part = head_split(packed, 1, model_width)
    values = head_split(packed, 2, model_width)
    key_form = layout.replace("l", "m")
    scores = (
        jnp.einsum(
            layout + "," + key_form + "->bhlm",
            queries,
            key_part,
            preferred_element_type=jnp.float32,
        )
        * factor
    )
    highest = jnp.max(scores, axis=-1, keepdims=True)
    expanded = jnp.exp(scores - highest)
    probs = expanded / jnp.sum(expanded, axis=-1, keepdims=True)
    return (widened, inv_rms, queries, key_part, values, probs, probs.astype(jnp.bfloat16), factor)


def forward_out(tokens_in, gain_vec, w_in, w_out, layout):
    widened, inv_rms, queries, key_part, values, probs, probs_b, factor = recompute(
        tokens_in, gain_vec, w_in, layout
    )
    key_form = layout.replace("l", "m")
    mixed = jnp.einsum(
        "bhlm," + key_form + "->" + layout, probs_b, values, preferred_element_type=jnp.float32
    )
    mixed = merge_heads(mixed.astype(jnp.bfloat16))
    return (widened + jnp.dot(mixed, w_out, preferred_element_type=jnp.float32)).astype(
        jnp.bfloat16
    )


def backward(tokens_in, upstream, gain_vec, w_in, w_out, layout):
    widened, inv_rms, queries, key_part, values, probs, probs_b, factor = recompute(
        tokens_in, gain_vec, w_in, layout
    )
    key_form = layout.replace("l", "m")
    d_mixed = jnp.dot(upstream, w_out.T, preferred_element_type=jnp.float32).astype(jnp.bfloat16)
    d_mixed = d_mixed.reshape(d_mixed.shape[:-1] + (H, d_mixed.shape[-1] // H))
    d_probs = jnp.einsum(
        layout + "," + key_form + "->bhlm", d_mixed, values, preferred_element_type=jnp.float32
    )
    d_values = jnp.einsum(
        "bhlm," + layout + "->" + key_form, probs_b, d_mixed, preferred_element_type=jnp.float32
    ).astype(jnp.bfloat16)
    centre = jnp.sum(probs * d_probs, axis=-1, keepdims=True)
    d_scores = (probs * (d_probs - centre) * factor).astype(jnp.bfloat16)
    d_queries = jnp.einsum(
        "bhlm," + key_form + "->" + layout, d_scores, key_part, preferred_element_type=jnp.float32
    ).astype(jnp.bfloat16)
    d_keys = jnp.einsum(
        "bhlm," + layout + "->" + key_form, d_scores, queries, preferred_element_type=jnp.float32
    ).astype(jnp.bfloat16)
    joined = jnp.concatenate(
        [merge_heads(d_queries), merge_heads(d_keys), merge_heads(d_values)], axis=-1
    )
    d_normed = jnp.dot(joined, w_in.T, preferred_element_type=jnp.float32)
    scaled = d_normed * gain_vec
    d_tokens = inv_rms * (
        scaled - widened * inv_rms * inv_rms * jnp.mean(scaled * widened, axis=-1, keepdims=True)
    )
    return (upstream.astype(jnp.float32) + d_tokens).astype(jnp.bfloat16)


def line_forward(lines, gain_vec, w_in, w_out):
    feature_count = lines.shape[3]
    flat = lines.reshape(-1, lines.shape[2], feature_count)
    return forward_out(flat, gain_vec, w_in, w_out, "blhe").reshape(lines.shape)


def line_backward(lines, upstream, gain_vec, w_in, w_out):
    feature_count = lines.shape[3]
    flat = lines.reshape(-1, lines.shape[2], feature_count)
    flat_up = upstream.reshape(flat.shape)
    return backward(flat, flat_up, gain_vec, w_in, w_out, "blhe").reshape(lines.shape)


def per_device(tokens, cotangent, gain_x, wqkv_x, wo_x, gain_z, wqkv_z, wo_z):
    full_in_x, full_out_x = (
        lax.all_gather(wqkv_x, "tr", axis=0, tiled=True),
        lax.all_gather(wo_x, "tr", axis=0, tiled=True),
    )
    full_in_z, full_out_z = (
        lax.all_gather(wqkv_z, "tr", axis=0, tiled=True),
        lax.all_gather(wo_z, "tr", axis=0, tiled=True),
    )
    width = tokens.shape[-1]
    lines = lax.all_to_all(tokens, "tr", split_axis=1, concat_axis=2, tiled=True)
    cot_lines = lax.all_to_all(cotangent, "tr", split_axis=1, concat_axis=2, tiled=True)
    cells = lines.shape[1] * lines.shape[2]
    flat = (lines.shape[0], cells, width)
    cot_columns = lax.all_to_all(
        cot_lines.reshape(flat), "gz", split_axis=1, concat_axis=0, tiled=True
    )
    mid_lines = line_forward(lines, gain_x, full_in_x, full_out_x)
    mid_columns = lax.all_to_all(
        mid_lines.reshape(flat), "gz", split_axis=1, concat_axis=0, tiled=True
    )
    grad_columns = backward(
        mid_columns, cot_columns, gain_z, full_in_z, full_out_z, "lbhe"
    )
    grad_lines = lax.all_to_all(grad_columns, "gz", split_axis=0, concat_axis=1, tiled=True)
    result_lines = line_backward(lines, grad_lines.reshape(lines.shape), gain_x, full_in_x, full_out_x)
    return lax.all_to_all(result_lines, "tr", split_axis=2, concat_axis=1, tiled=True)


F32, BF16 = jnp.float32, jnp.bfloat16


def nt(a, b):
    return lax.dot_general(a, b, (((1,), (1,)), ((), ())), preferred_element_type=F32)


def tn(a, b):
    return lax.dot_general(a, b, (((0,), (0,)), ((), ())), preferred_element_type=F32)


def nn(a, b):
    return jnp.dot(a, b, preferred_element_type=F32)


def rms(a):
    return lax.rsqrt(jnp.mean(a * a, axis=-1, keepdims=True) + 1e-06)


def project(a, rstd, gain, w, qkv):
    width = a.shape[1]
    normed = (a * rstd * gain).astype(BF16)
    for j in range(3):
        cols = slice(j * width, (j + 1) * width)
        qkv[:, cols] = nn(normed, w[:, cols]).astype(BF16)


def line_mask(block, line, inner):
    key = lax.broadcasted_iota(jnp.int32, (block, block), 0)
    query = lax.broadcasted_iota(jnp.int32, (block, block), 1)
    if inner:
        return key % line == query % line
    return key // line == query // line


def head_spans(width):
    size = width // H
    return [[pl.ds(n * width + h * size, size) for n in range(3)] for h in range(H)]


def softmax_rows(qkv, at, spans, mask, factor):
    qk = [nt(qkv[at, sp[1]], qkv[at, sp[0]]) for sp in spans]
    scores = [jnp.where(mask, x * factor, -1e30) for x in qk]
    tops = [jnp.max(x, axis=0, keepdims=True) for x in scores]
    grown = [jnp.exp(x - t) for x, t in zip(scores, tops)]
    sums = [1.0 / jnp.sum(x, axis=0, keepdims=True) for x in grown]
    return [x * t for x, t in zip(grown, sums)]


def attend_forward(qkv, probs, first, mixed, mask):
    rows, width = mixed.shape
    block = mask.shape[0]
    factor = 1.0 / math.sqrt(width // H)
    spans = head_spans(width)
    for b in range(rows // block):
        at = pl.ds(b * block, block)
        ps = softmax_rows(qkv, at, spans, mask, factor)
        for h, p in enumerate(ps):
            probs[(first + b) * H + h] = p
        outs = [tn(p.astype(BF16), qkv[at, sp[2]]) for p, sp in zip(ps, spans)]
        for sp, o in zip(spans, outs):
            mixed[at, sp[0]] = o.astype(BF16)


def attend_backward(qkv, probs, first, d_mixed, joined, mask, keep):
    rows, width = d_mixed.shape
    block = mask.shape[0]
    factor = 1.0 / math.sqrt(width // H)
    spans = head_spans(width)
    for b in range(rows // block):
        at = pl.ds(b * block, block)
        dps = [nt(qkv[at, sp[2]], d_mixed[at, sp[0]]) for sp in spans]
        if keep:
            ps = [probs[(first + b) * H + h] for h in range(H)]
        else:
            ps = softmax_rows(qkv, at, spans, mask, factor)
        dvs = [nn(p.astype(BF16), d_mixed[at, sp[0]]) for p, sp in zip(ps, spans)]
        centres = [jnp.sum(p * dp, axis=0, keepdims=True) for p, dp in zip(ps, dps)]
        dss = [(p * (dp - c) * factor).astype(BF16) for p, dp, c in zip(ps, dps, centres)]
        dks = [nn(ds, qkv[at, sp[0]]) for ds, sp in zip(dss, spans)]
        dqs = [tn(ds, qkv[at, sp[1]]) for ds, sp in zip(dss, spans)]
        for sp, dq, dk, dv in zip(spans, dqs, dks, dvs):
            joined[at, sp[0]] = dq.astype(BF16)
            joined[at, sp[1]] = dk.astype(BF16)
            joined[at, sp[2]] = dv.astype(BF16)


def norm_backward(a, c, rstd, gain, joined, w, dn):
    width = a.shape[-1]
    part = width // 3
    for j in range(3):
        dn[:, j * part : (j + 1) * part] = nt(joined[...], w[j * part : (j + 1) * part, :])
    scaled = dn[...] * gain
    mean = jnp.mean(scaled * a, axis=-1, keepdims=True)
    return (c + rstd * (scaled - a * (rstd * rstd) * mean)).astype(BF16)


def kernel(
    nt_, ng, line_x,
    tok, cot, gain_x, wx, ox, gain_z, wz, oz, out,
    tokr, cotr, cotz, mids, midr, grads, gradr, outs,
    fwx, fox, fwz, foz, qkvx, qkvz, probs, mixed, dmix, joined, dn, ax, az, cz,
    tr_send, tr_recv, gz_send, gz_recv, w_send, w_recv, local,
):
    me, mine = lax.axis_index("tr"), lax.axis_index("gz")
    sib, across = me + 1 - 2 * (me % 2), (me + 2) % nt_
    gy, gp = mine % 2, (mine // 2) % 2
    ynbr, znbr = mine + 1 - 2 * gy, mine + 2 - 4 * gp
    slab, pairs, width = tok.shape[0], tok.shape[3], tok.shape[5]
    parts = tok.shape[2]
    half = ax.shape[0] // parts
    block = half // 2

    barrier = pltpu.get_barrier_semaphore()
    for d in range(1, nt_):
        pl.semaphore_signal(barrier, inc=1, device_id=((me + d) % nt_, mine), device_id_type=pl.DeviceIdType.MESH)
    for d in range(1, ng):
        pl.semaphore_signal(barrier, inc=1, device_id=(me, (mine + d) % ng), device_id_type=pl.DeviceIdType.MESH)

    own_w = ((wx, wx, wx, ox), (wz, wz, wz, oz))
    full_w = ((fwx, fwx, fwx, fox), (fwz, fwz, fwz, foz))
    depth = wx.shape[0]
    quarter = depth // 4

    here = [
        pltpu.make_async_copy(tok.at[:, me], tokr.at[:, :, :, me], local.at[0]),
        pltpu.make_async_copy(cot.at[:, me], cotr.at[:, :, :, me // 2, me % 2], local.at[1]),
    ]
    for s in range(2):
        for k in (0, 3):
            to = full_w[s][k].at[pl.ds(pl.multiple_of(me * depth, 16), depth)]
            here.append(pltpu.make_async_copy(own_w[s][k], to, local.at[len(here)]))
    for copy in here:
        copy.start()

    pl.semaphore_wait(barrier, nt_ + ng - 2)

    def remote(src, dst, send, recv, t, g):
        return pltpu.make_async_remote_copy(
            src_ref=src, dst_ref=dst, send_sem=send, recv_sem=recv,
            device_id=(t, g), device_id_type=pl.DeviceIdType.MESH,
        )

    def own(s, k, row, n):
        at = pl.ds(pl.multiple_of(row, 16), n)
        return own_w[s][k].at[at, pl.ds((k % 3) * width, width)]

    def spot(s, k, shard, row, n):
        at = pl.ds(pl.multiple_of(shard * depth + row, 16), n)
        return full_w[s][k].at[at, pl.ds((k % 3) * width, width)]

    def push(s, k, role, src, dst, t, g):
        return remote(src, dst, w_send.at[s, k, role], w_recv.at[s, k, role], t, g)

    q_me, q_y = (2 * gy + gp) * quarter, (2 - 2 * gy + gp) * quarter
    q_z, q_d = (2 * gy + 1 - gp) * quarter, (3 - 2 * gy - gp) * quarter
    by_z = (0, 1)

    def direct_rows(s, k):
        if s == 0:
            return q_me, quarter
        n = DIRECT[k] * quarter
        return gy * (depth - n), n

    def relay_rows(s, k, y):
        if s == 0:
            return (2 * (1 - y) + gp) * quarter, quarter
        n = DIRECT[k] * quarter
        return (1 - y) * n, depth - n

    def role0(s, k):
        row, n = direct_rows(s, k)
        return push(s, k, 0, own(s, k, row, n), spot(s, k, me, row, n), across, mine)

    def role1(s, k):
        return push(s, k, 1, own(s, k, 0, depth), spot(s, k, me, 0, depth), sib, mine)

    def role2(s, k):
        row, n = relay_rows(s, k, 1 - gy)
        at = spot(s, k, across, row, n)
        return push(s, k, 2, at, at, me, ynbr)

    def role3(k):
        at = spot(0, k, across, q_me, quarter)
        return push(0, k, 3, at, at, me, znbr)

    def role4(k):
        if k in by_z:
            at = spot(0, k, across, q_y, quarter)
            return push(0, k, 4, at, at, me, znbr)
        at = spot(0, k, across, q_z, quarter)
        return push(0, k, 4, at, at, me, ynbr)

    def role5(s, k):
        at = spot(s, k, across, 0, depth)
        return push(s, k, 5, at, at, sib, mine)

    def arrived(s, k, role):
        if role == 0:
            at = spot(s, k, across, *direct_rows(s, k))
        elif role == 1:
            at = spot(s, k, sib, 0, depth)
        elif role == 2:
            at = spot(s, k, across, *relay_rows(s, k, gy))
        elif role == 3:
            at = spot(0, k, across, q_z, quarter)
        elif role == 4:
            at = spot(0, k, across, q_d, quarter)
        else:
            at = spot(s, k, (sib + 2) % nt_, 0, depth)
        push(s, k, role, at, at, sib, mine).wait_recv()

    def tr_copy(n, d):
        t = (me + d) % nt_
        src, dst = tr_ends(n, t, me)
        return remote(src, dst, tr_send.at[n, d], tr_recv.at[n, d], t, mine)

    def tr_ends(n, to, source):
        if n == 0:
            return tok.at[:, to], tokr.at[:, :, :, source]
        if n == 1:
            return cot.at[:, to], cotr.at[:, :, :, source // 2, source % 2]
        return outs.at[n - 2, :, :, to], out.at[:, source, n - 2]

    def gz_ends(n, to, source):
        if n == 0:
            return cotr.at[:, :, to // 2, :, to % 2], cotz.at[pl.ds(source * slab, slab)]
        if n <= 2:
            h = n - 1
            return mids.at[h, :, to // 2, :, to % 2], midr.at[h, pl.ds(source * slab, slab)]
        h = n - 3
        return grads.at[h, pl.ds(to * slab, slab)], gradr.at[h, :, source // 2, :, source % 2]

    def gz_copy(n, d):
        g = (mine + d) % ng
        src, dst = gz_ends(n, g, mine)
        return remote(src, dst, gz_send.at[n, d], gz_recv.at[n, d], me, g)

    far_first = [2, 3, 1] if nt_ == 4 else list(range(1, nt_))
    gz_order = sorted(range(1, ng), key=lambda d: -min(d, ng - d))

    def tr_begin(n):
        for d in far_first:
            tr_copy(n, d).start()

    def tr_end(n):
        for d in range(1, nt_):
            tr_copy(n, d).wait_send()
            src = (me + nt_ - d) % nt_
            at = tr_ends(n, me, src)[1]
            remote(at, at, tr_send.at[n, d], tr_recv.at[n, d], src, mine).wait_recv()

    def gz_begin(n):
        for d in gz_order:
            gz_copy(n, d).start()

    def gz_end(n):
        for d in range(1, ng):
            gz_copy(n, d).wait_send()
            src = (mine + ng - d) % ng
            at = gz_ends(n, mine, src)[1]
            remote(at, at, gz_send.at[n, d], gz_recv.at[n, d], me, src).wait_recv()

    ks = range(4)

    for k in ks:
        role0(0, k).start()
    for k in ks:
        role1(0, k).start()
    for k in ks:
        arrived(0, k, 0)
        role2(0, k).start()
        role3(k).start()
        if k == TOK_AFTER:
            tr_begin(0)
    for k in ks:
        arrived(0, k, 2)
        if k in by_z:
            role4(k).start()
        arrived(0, k, 3)
        if k not in by_z:
            role4(k).start()
    for k in ks:
        arrived(0, k, 4)
        role5(0, k).start()
    for copy in here:
        copy.wait()
    tr_end(0)
    tr_begin(1)
    for k in ks:
        role0(1, k).start()
    for k in ks:
        role1(1, k).start()
    for h in range(parts):
        ax[pl.ds(h * half, half)] = tokr[:, h].reshape(half, width)
    for k in ks:
        arrived(0, k, 1)
        arrived(0, k, 5)

    def relay_z(pieces):
        for k in pieces:
            arrived(1, k, 0)
            role2(1, k).start()

    mask_x = line_mask(block, line_x, False)
    mask_z = line_mask(block, block // (slab * ng), True)
    gx, gz = gain_x[...][None], gain_z[...][None]
    rstd_x = []
    for h in range(parts):
        at = pl.ds(h * half, half)
        a = ax[at].astype(F32)
        rstd_x.append(rms(a))
        project(a, rstd_x[h], gx, fwx, qkvx.at[at])
        attend_forward(qkvx.at[at], probs, 2 * h, mixed.at[at], mask_x)
        mid = ax[at].astype(F32) + nn(mixed[at], fox[...])
        mids[h] = mid.astype(BF16).reshape(mids.shape[1:])
        gz_begin(1 + h)
        midr[h, pl.ds(mine * slab, slab)] = mids[h, :, mine // 2, :, mine % 2]
        if h == 0:
            tr_end(1)
            gz_begin(0)
            cotz[pl.ds(mine * slab, slab)] = cotr[:, :, mine // 2, :, mine % 2]
            relay_z((0,))
    relay_z((1, 2, 3))
    for k in ks:
        arrived(1, k, 2)
        role5(1, k).start()
    for k in ks:
        arrived(1, k, 1)
        arrived(1, k, 5)
    gz_end(0)

    for h in range(parts):
        at = pl.ds(h * half, half)
        for j in range(2):
            cz[pl.ds(h * half + j * block, block)] = cotz[:, h, j].reshape(block, width)
        dmix[at] = nt(cz[at], foz[...]).astype(BF16)
    for h in range(parts):
        at = pl.ds(h * half, half)
        gz_end(1 + h)
        for j in range(2):
            az[pl.ds(h * half + j * block, block)] = midr[h, :, j].reshape(block, width)
        a = az[at].astype(F32)
        rstd = rms(a)
        project(a, rstd, gz, fwz, qkvz.at[at])
        attend_backward(qkvz.at[at], probs, 0, dmix.at[at], joined.at[at], mask_z, False)
        back = norm_backward(
            az[at].astype(F32), cz[at].astype(F32), rstd, gz, joined.at[at], fwz, dn.at[at]
        )
        for j in range(2):
            grads[h, :, j] = back[j * block : (j + 1) * block].reshape(slab * ng, block // (slab * ng), width)
        gz_begin(3 + h)
        gradr[h, :, mine // 2, :, mine % 2] = grads[h, pl.ds(mine * slab, slab)]

    kept = []
    for h in range(parts):
        at = pl.ds(h * half, half)
        gz_end(3 + h)
        c = gradr[h].reshape(half, width)
        dmix[at] = nt(c, fox[...]).astype(BF16)
        attend_backward(qkvx.at[at], probs, 2 * h, dmix.at[at], joined.at[at], mask_x, True)
        back = norm_backward(
            ax[at].astype(F32), c.astype(F32), rstd_x[h], gx, joined.at[at], fwx, dn.at[at]
        )
        outs[h] = back.reshape(outs.shape[1:])
        tr_begin(2 + h)
        keep = pltpu.make_async_copy(outs.at[h, :, :, me], out.at[:, me, h], local.at[6 + h])
        keep.start()
        kept.append(keep)

    for k in ks:
        for s in range(2):
            role0(s, k).wait_send()
            role1(s, k).wait_send()
            role2(s, k).wait_send()
            role5(s, k).wait_send()
        role3(k).wait_send()
        role4(k).wait_send()
    for h in range(parts):
        tr_end(2 + h)
        kept[h].wait()


DIRECT = (2, 2, 3, 3)
TOK_AFTER = 1


def fits_kernel(trs, gzs, slab, y, x_own, width, depth):
    return (trs, gzs, y, x_own) == (4, 8, 32, 2) and (slab * trs * x_own * 4) % 32 == 0 and width % 128 == 0 and depth % 64 == 0


def fused(trs, gzs, tokens, cotangent, gain_x, wqkv_x, wo_x, gain_z, wqkv_z, wo_z):
    slab, y, x_own, width = tokens.shape
    x, z = x_own * trs, slab * gzs
    rows = slab * y * x_own
    parts, group = 2, gzs // 2
    split = (slab, trs, parts, group, x_own, width)
    block = rows // 4
    lines = (slab, group, 2, trs // 2, x_own, width)
    vm = pl.BlockSpec(memory_space=pltpu.VMEM)
    hbm = pl.BlockSpec(memory_space=pl.ANY)
    wide = wqkv_x.shape[1]
    result = pl.pallas_call(
        functools.partial(kernel, trs, gzs, x),
        out_shape=jax.ShapeDtypeStruct(split, BF16),
        in_specs=[hbm, hbm, vm, hbm, hbm, vm, hbm, hbm],
        out_specs=hbm,
        scratch_shapes=[
            pltpu.VMEM((slab, parts, group, trs, x_own, width), BF16),
            pltpu.VMEM((slab, parts, group, 2, trs // 2, x_own, width), BF16),
            pltpu.VMEM((z, parts, 2, x_own, width), BF16),
            pltpu.VMEM((parts, *lines), BF16),
            pltpu.VMEM((parts, z, 2, x_own, width), BF16),
            pltpu.VMEM((parts, z, 2, x_own, width), BF16),
            pltpu.VMEM((parts, *lines), BF16),
            pltpu.VMEM((parts, slab, group, trs, x_own, width), BF16),
        ]
        + [pltpu.VMEM((width, wide), BF16), pltpu.VMEM((width, width), BF16)] * 2
        + [pltpu.VMEM((rows, wide), BF16)] * 2
        + [pltpu.VMEM((4 * H, block, block), F32)]
        + [pltpu.VMEM((rows, width), BF16)] * 2
        + [pltpu.VMEM((rows, wide), BF16), pltpu.VMEM((rows, width), F32)]
        + [pltpu.VMEM((rows, width), BF16)] * 3
        + [
            pltpu.SemaphoreType.DMA((4, trs)),
            pltpu.SemaphoreType.DMA((4, trs)),
            pltpu.SemaphoreType.DMA((5, gzs)),
            pltpu.SemaphoreType.DMA((5, gzs)),
            pltpu.SemaphoreType.DMA((2, 4, 6)),
            pltpu.SemaphoreType.DMA((2, 4, 6)),
            pltpu.SemaphoreType.DMA((8,)),
        ],
        compiler_params=pltpu.CompilerParams(
            collective_id=0, has_side_effects=True, vmem_limit_bytes=56 * 1024 * 1024
        ),
    )(
        tokens.reshape(split), cotangent.reshape(split),
        gain_x, wqkv_x, wo_x, gain_z, wqkv_z, wo_z,
    )
    return result.reshape(tokens.shape)


def solution(mesh):
    trs, gzs = mesh.shape["tr"], mesh.shape["gz"]

    def body(tokens, *rest):
        if fits_kernel(trs, gzs, *tokens.shape, rest[2].shape[0]):
            return fused(trs, gzs, tokens, *rest)
        return per_device(tokens, *rest)

    return jax.shard_map(
        body,
        mesh=mesh,
        in_specs=(
            P("gz", None, "tr", None),
            P("gz", None, "tr", None),
            P(),
            P("tr", None),
            P("tr", None),
            P(),
            P("tr", None),
            P("tr", None),
        ),
        out_specs=P("gz", None, "tr", None),
        check_vma=False,
    )
```

time: 96 us -> 79 us (0.82)
  Pallas kernels: 90.1 us -> 76.2 us
  local copies, waits for them, and re-layouts: 5.01 us -> 2.15 us
    pallas_call x1, Pallas kernels: 90.1 us -> 76.2 us  [fused(): pl.pallas_call(functools.partial(kernel, trs, gzs, x), out_shape=jax.Shap...]
    reshape x3 -> x0, local copies, waits for them, and re-layouts: 5.01 us -> none  [the longest x1 2.05 us: fused(): tokens.reshape(split)]
    unnamed x2 -> x1, local copies, waits for them, and re-layouts: 0.01 us -> 2.15 us
where the time goes in v1:
time: 79 us; the launch traced here: 78.3 us
  Pallas kernels  76.2 us (96%)
  local copies, waits for them, and re-layouts  2.15 us (3%)
    pallas_call x1, Pallas kernels, fused(): pl.pallas_call(functools.partial(kernel, trs, gzs, x), out_shape=jax.Shap...  76.2 us
    unnamed x1, local copies, waits for them, and re-layouts  2.15 us

profile of v1, /device:TPU:0, one launch (start us, length us, event | category | flops | bytes accessed | tf_op | source)
XLA Modules:
  0.0 78.3 jit_solution(15293840918686453104)
XLA Ops:
  0.0 76.2 %shard_map.82 = bf16[5,4,2,4,2,768]{5,4,3,2,1,0:T(2,128)(2,1)} custom-call(bf16[5,4,2,4,2,768]{5,4,3,2,1,0:T(2,128)(2,1)} %bitcast.4, bf16[5,4,2,4,2,768]{5,4,3,2,1,0:T(2,128)(2,1)} %bitcast.5, f32[768]{0:T(1024)} %gain_x.1, bf16[192,2304]{1,0:T(8,128)(2,1)} %wx.1, bf16[192,768]{1,0:T(8,128)(2,1)} %ox.1, f32[768]{0:T(1024)} %gain_z.1, bf16[192,2304]{1,0:T(8,128)(2,1)} %wz.1, ...), custom_call_target="tpu_custom_call" | custom-call | tf_op jit(solution)/shard_map/pallas_call | solution.py:540
  76.2 2.1 %copy.10 = bf16[5,32,2,768]{3,2,1,0:T(2,128)(2,1)} copy(bf16[5,32,2,768]{3,2,1,0:T(2,128)(2,1)} %bitcast.3) | data formatting | bytes 983040

commit v2 on v1

--- a/solution.py
+++ b/solution.py
@@ -184,6 +184,17 @@
     return [x * t for x, t in zip(grown, sums)]
 
 
+def attend_scores(qkv, probs, first, mask):
+    rows = qkv.shape[0]
+    width = qkv.shape[1] // 3
+    block = mask.shape[0]
+    factor = 1.0 / math.sqrt(width // H)
+    for b in range(rows // block):
+        ps = softmax_rows(qkv, pl.ds(b * block, block), head_spans(width), mask, factor)
+        for h, p in enumerate(ps):
+            probs[(first + b) * H + h] = p
+
+
 def attend_forward(qkv, probs, first, mixed, mask):
     rows, width = mixed.shape
     block = mask.shape[0]
@@ -199,18 +210,15 @@
             mixed[at, sp[0]] = o.astype(BF16)
 
 
-def attend_backward(qkv, probs, first, d_mixed, joined, mask, keep):
+def attend_backward(qkv, probs, first, d_mixed, joined):
     rows, width = d_mixed.shape
-    block = mask.shape[0]
+    block = probs.shape[1]
     factor = 1.0 / math.sqrt(width // H)
     spans = head_spans(width)
     for b in range(rows // block):
         at = pl.ds(b * block, block)
         dps = [nt(qkv[at, sp[2]], d_mixed[at, sp[0]]) for sp in spans]
-        if keep:
-            ps = [probs[(first + b) * H + h] for h in range(H)]
-        else:
-            ps = softmax_rows(qkv, at, spans, mask, factor)
+        ps = [probs[(first + b) * H + h] for h in range(H)]
         dvs = [nn(p.astype(BF16), d_mixed[at, sp[0]]) for p, sp in zip(ps, spans)]
         centres = [jnp.sum(p * dp, axis=0, keepdims=True) for p, dp in zip(ps, dps)]
         dss = [(p * (dp - c) * factor).astype(BF16) for p, dp, c in zip(ps, dps, centres)]
@@ -235,9 +243,9 @@
 def kernel(
     nt_, ng, line_x,
     tok, cot, gain_x, wx, ox, gain_z, wz, oz, out,
-    tokr, cotr, cotz, mids, midr, grads, gradr, outs,
-    fwx, fox, fwz, foz, qkvx, qkvz, probs, mixed, dmix, joined, dn, ax, az, cz,
-    tr_send, tr_recv, gz_send, gz_recv, w_send, w_recv, local,
+    tokr, cotz, mids, midr, grads, gradr, outs,
+    fwx, fox, fwz, foz, qkvx, qkvz, probs, probz, mixed, dmix, joined, dn, ax, az, cz,
+    tr_send, tr_recv, gz_send, gz_recv, w_send, w_recv, c_send, c_recv, entered, local,
 ):
     me, mine = lax.axis_index("tr"), lax.axis_index("gz")
     sib, across = me + 1 - 2 * (me % 2), (me + 2) % nt_
@@ -248,11 +256,29 @@
     half = ax.shape[0] // parts
     block = half // 2
 
+    def tell(sem, t, g):
+        pl.semaphore_signal(sem, inc=1, device_id=(t, g), device_id_type=pl.DeviceIdType.MESH)
+
+    zrow, last = mine // 2, ng // 2 - 1
+
+    def tell_lanes(sem):
+        for d in range(1, nt_):
+            tell(sem, (me + d) % nt_, mine)
+
+    def tell_near(sem):
+        tell(sem, me, ynbr)
+        pl.when(zrow > 0)(lambda: tell(sem, me, mine - 2))
+        pl.when(zrow < last)(lambda: tell(sem, me, mine + 2))
+
+    near = 1 + (zrow + last) // (last + 1) + (2 * last - zrow) // (last + 1)
+
     barrier = pltpu.get_barrier_semaphore()
-    for d in range(1, nt_):
-        pl.semaphore_signal(barrier, inc=1, device_id=((me + d) % nt_, mine), device_id_type=pl.DeviceIdType.MESH)
-    for d in range(1, ng):
-        pl.semaphore_signal(barrier, inc=1, device_id=(me, (mine + d) % ng), device_id_type=pl.DeviceIdType.MESH)
+    tell_lanes(barrier)
+    if NEAR:
+        tell_near(barrier)
+    else:
+        for d in range(1, ng):
+            tell(barrier, me, (mine + d) % ng)
 
     own_w = ((wx, wx, wx, ox), (wz, wz, wz, oz))
     full_w = ((fwx, fwx, fwx, fox), (fwz, fwz, fwz, foz))
@@ -261,7 +287,6 @@
 
     here = [
         pltpu.make_async_copy(tok.at[:, me], tokr.at[:, :, :, me], local.at[0]),
-        pltpu.make_async_copy(cot.at[:, me], cotr.at[:, :, :, me // 2, me % 2], local.at[1]),
     ]
     for s in range(2):
         for k in (0, 3):
@@ -270,7 +295,23 @@
     for copy in here:
         copy.start()
 
-    pl.semaphore_wait(barrier, nt_ + ng - 2)
+    if NEAR:
+        pl.semaphore_wait(barrier, nt_ - 1 + near)
+        tell_near(entered.at[0])
+    else:
+        pl.semaphore_wait(barrier, nt_ + ng - 2)
+        tell_lanes(entered.at[3])
+
+    def widen(step):
+        if step < 3:
+            if NEAR:
+                pl.semaphore_wait(entered.at[step], near)
+                if step < 2:
+                    tell_near(entered.at[step + 1])
+                else:
+                    tell_lanes(entered.at[3])
+        else:
+            pl.semaphore_wait(entered.at[3], nt_ - 1)
 
     def remote(src, dst, send, recv, t, g):
         return pltpu.make_async_remote_copy(
@@ -289,21 +330,27 @@
     def push(s, k, role, src, dst, t, g):
         return remote(src, dst, w_send.at[s, k, role], w_recv.at[s, k, role], t, g)
 
-    q_me, q_y = (2 * gy + gp) * quarter, (2 - 2 * gy + gp) * quarter
-    q_z, q_d = (2 * gy + 1 - gp) * quarter, (3 - 2 * gy - gp) * quarter
+    odd = (gy + gp) % 2
+    q_me, q_d = (2 * odd + gy) * quarter, (2 * odd + 1 - gy) * quarter
+    q_y, q_z = (3 - 2 * odd - gy) * quarter, (2 - 2 * odd + gy) * quarter
     by_z = (0, 1)
 
     def direct_rows(s, k):
-        if s == 0:
+        if s == 0 or DIRECT[k] == 0:
             return q_me, quarter
+        if DIRECT[k] == 1:
+            return 2 * odd * quarter, 2 * quarter
         n = DIRECT[k] * quarter
         return gy * (depth - n), n
 
-    def relay_rows(s, k, y):
-        if s == 0:
-            return (2 * (1 - y) + gp) * quarter, quarter
+    def relay_rows(s, k, sent):
+        if s == 0 or DIRECT[k] <= 1:
+            return (q_me if sent else q_y), quarter
         n = DIRECT[k] * quarter
-        return (1 - y) * n, depth - n
+        return (gy if sent else 1 - gy) * n, depth - n
+
+    def over_z(s, k):
+        return s == 0 or DIRECT[k] <= 1
 
     def role0(s, k):
         row, n = direct_rows(s, k)
@@ -313,20 +360,23 @@
         return push(s, k, 1, own(s, k, 0, depth), spot(s, k, me, 0, depth), sib, mine)
 
     def role2(s, k):
-        row, n = relay_rows(s, k, 1 - gy)
+        row, n = relay_rows(s, k, True)
         at = spot(s, k, across, row, n)
         return push(s, k, 2, at, at, me, ynbr)
 
-    def role3(k):
-        at = spot(0, k, across, q_me, quarter)
-        return push(0, k, 3, at, at, me, znbr)
-
-    def role4(k):
+    def role3(s, k):
+        at = spot(s, k, across, q_me, quarter)
+        return push(s, k, 3, at, at, me, znbr)
+
+    def role4(s, k):
         if k in by_z:
-            at = spot(0, k, across, q_y, quarter)
-            return push(0, k, 4, at, at, me, znbr)
-        at = spot(0, k, across, q_z, quarter)
-        return push(0, k, 4, at, at, me, ynbr)
+            at = spot(s, k, across, q_y, quarter)
+            return push(s, k, 4, at, at, me, znbr)
+        at = spot(s, k, across, q_z, quarter)
+        return push(s, k, 4, at, at, me, ynbr)
+
+    def two_steps(s, k):
+        return s == 0 or DIRECT[k] == 0
 
     def role5(s, k):
         at = spot(s, k, across, 0, depth)
@@ -338,11 +388,11 @@
         elif role == 1:
             at = spot(s, k, sib, 0, depth)
         elif role == 2:
-            at = spot(s, k, across, *relay_rows(s, k, gy))
+            at = spot(s, k, across, *relay_rows(s, k, False))
         elif role == 3:
-            at = spot(0, k, across, q_z, quarter)
+            at = spot(s, k, across, q_z, quarter)
         elif role == 4:
-            at = spot(0, k, across, q_d, quarter)
+            at = spot(s, k, across, q_d, quarter)
         else:
             at = spot(s, k, (sib + 2) % nt_, 0, depth)
         push(s, k, role, at, at, sib, mine).wait_recv()
@@ -355,17 +405,13 @@
     def tr_ends(n, to, source):
         if n == 0:
             return tok.at[:, to], tokr.at[:, :, :, source]
-        if n == 1:
-            return cot.at[:, to], cotr.at[:, :, :, source // 2, source % 2]
-        return outs.at[n - 2, :, :, to], out.at[:, source, n - 2]
+        return outs.at[n - 1, :, :, to], out.at[:, source, n - 1]
 
     def gz_ends(n, to, source):
-        if n == 0:
-            return cotr.at[:, :, to // 2, :, to % 2], cotz.at[pl.ds(source * slab, slab)]
-        if n <= 2:
-            h = n - 1
+        if n < 2:
+            h = n
             return mids.at[h, :, to // 2, :, to % 2], midr.at[h, pl.ds(source * slab, slab)]
-        h = n - 3
+        h = n - 2
         return grads.at[h, pl.ds(to * slab, slab)], gradr.at[h, :, source // 2, :, source % 2]
 
     def gz_copy(n, d):
@@ -398,34 +444,99 @@
             at = gz_ends(n, mine, src)[1]
             remote(at, at, gz_send.at[n, d], gz_recv.at[n, d], me, src).wait_recv()
 
+    core, zc, zs = me % 2, mine // 2, ng // 2
+    lanes = (me, sib, across, (sib + 2) % nt_)
+
+    def cot_copy(j, dz, only_at=None):
+        z = (zc + dz) % zs
+        src = cot.at[:, lanes[j], :, z]
+        dst = cotz.at[pl.ds(mine * slab, slab), :, me // 2]
+        return remote(src, dst, c_send.at[j, dz], c_recv.at[j, dz, gy], lanes[j], 2 * z + core)
+
+    def unless_self(j, dz, test, act):
+        if j == 0 and dz == 0:
+            pl.when(test)(act)
+        else:
+            act()
+
+    def cot_begin(js):
+        for dz in (2, 1, 3, 0):
+            for j in js:
+                unless_self(j, dz, core != gy, lambda: cot_copy(j, dz).start())
+
+    def cot_end():
+        for dz in range(zs):
+            for j in range(4):
+                unless_self(j, dz, core != gy, lambda: cot_copy(j, dz).wait_send())
+        other = (core + gy) % 2
+        for i in range(2):
+            at_x = (me // 2 + i) % 2
+            for dz in range(zs):
+                for ys in range(2):
+                    g = 2 * ((zc + zs - dz) % zs) + ys
+                    at = cotz.at[pl.ds(g * slab, slab), :, at_x]
+                    copy = remote(at, at, c_send.at[0, 0], c_recv.at[other + 2 * i, dz, ys], sib, mine)
+                    if i == 0 and dz == 0:
+                        pl.when((core != gy) | (gy != ys))(lambda: copy.wait_recv())
+                    else:
+                        copy.wait_recv()
+        pl.when(core == gy)(lambda: cot_self().wait())
+
+    def cot_self():
+        return pltpu.make_async_copy(cot.at[:, me, :, zc], cotz.at[pl.ds(mine * slab, slab), :, me // 2], local.at[7])
+
     ks = range(4)
 
+    def begin_w1(pieces):
+        for k in pieces:
+            role0(1, k).start()
+
     for k in ks:
         role0(0, k).start()
     for k in ks:
         role1(0, k).start()
+    pl.when(core == gy)(lambda: cot_self().start())
+    for step in range(3):
+        widen(step)
+    if COT0 == 0:
+        cot_begin((0,))
+    if WIDE == 0:
+        widen(3)
+        cot_begin((1,))
     for k in ks:
         arrived(0, k, 0)
         role2(0, k).start()
-        role3(k).start()
+        role3(0, k).start()
+        if k == 0 and WIDE == 1:
+            widen(3)
+            if COT0 == 0:
+                cot_begin((1,))
         if k == TOK_AFTER:
             tr_begin(0)
+        begin_w1([j for j in ks if W1_AT[j] == k])
+        if COT1 == k:
+            cot_begin((2, 3))
     for k in ks:
         arrived(0, k, 2)
         if k in by_z:
-            role4(k).start()
+            role4(0, k).start()
         arrived(0, k, 3)
         if k not in by_z:
-            role4(k).start()
+            role4(0, k).start()
+    if COT0 == 4:
+        cot_begin((0, 1))
+    begin_w1([j for j in ks if W1_AT[j] == 4])
+    if COT1 == 4:
+        cot_begin((2, 3))
     for k in ks:
         arrived(0, k, 4)
         role5(0, k).start()
     for copy in here:
         copy.wait()
     tr_end(0)
-    tr_begin(1)
-    for k in ks:
-        role0(1, k).start()
+    begin_w1([j for j in ks if W1_AT[j] == 5])
+    if COT1 == 5:
+        cot_begin((2, 3))
     for k in ks:
         role1(1, k).start()
     for h in range(parts):
@@ -438,6 +549,8 @@
         for k in pieces:
             arrived(1, k, 0)
             role2(1, k).start()
+            if over_z(1, k):
+                role3(1, k).start()
 
     mask_x = line_mask(block, line_x, False)
     mask_z = line_mask(block, block // (slab * ng), True)
@@ -451,57 +564,68 @@
         attend_forward(qkvx.at[at], probs, 2 * h, mixed.at[at], mask_x)
         mid = ax[at].astype(F32) + nn(mixed[at], fox[...])
         mids[h] = mid.astype(BF16).reshape(mids.shape[1:])
-        gz_begin(1 + h)
+        gz_begin(h)
         midr[h, pl.ds(mine * slab, slab)] = mids[h, :, mine // 2, :, mine % 2]
         if h == 0:
-            tr_end(1)
-            gz_begin(0)
-            cotz[pl.ds(mine * slab, slab)] = cotr[:, :, mine // 2, :, mine % 2]
-            relay_z((0,))
-    relay_z((1, 2, 3))
+            relay_z(RELAY1)
+    relay_z([k for k in ks if k not in RELAY1])
     for k in ks:
         arrived(1, k, 2)
-        role5(1, k).start()
+        if over_z(1, k):
+            arrived(1, k, 3)
+        if two_steps(1, k):
+            role4(1, k).start()
+        else:
+            role5(1, k).start()
+    for k in ks:
+        if two_steps(1, k):
+            arrived(1, k, 4)
+            role5(1, k).start()
     for k in ks:
         arrived(1, k, 1)
         arrived(1, k, 5)
-    gz_end(0)
-
-    for h in range(parts):
+
+    def z_front(h):
         at = pl.ds(h * half, half)
-        for j in range(2):
-            cz[pl.ds(h * half + j * block, block)] = cotz[:, h, j].reshape(block, width)
-        dmix[at] = nt(cz[at], foz[...]).astype(BF16)
-    for h in range(parts):
-        at = pl.ds(h * half, half)
-        gz_end(1 + h)
+        gz_end(h)
         for j in range(2):
             az[pl.ds(h * half + j * block, block)] = midr[h, :, j].reshape(block, width)
         a = az[at].astype(F32)
         rstd = rms(a)
         project(a, rstd, gz, fwz, qkvz.at[at])
-        attend_backward(qkvz.at[at], probs, 0, dmix.at[at], joined.at[at], mask_z, False)
+        attend_scores(qkvz.at[at], probz, 2 * h, mask_z)
+        return rstd
+
+    for h in range(parts):
+        at = pl.ds(h * half, half)
+        rstd = z_front(h)
+        if h == 0:
+            cot_end()
+        for j in range(2):
+            cz[pl.ds(h * half + j * block, block)] = cotz[:, h, j].reshape(block, width)
+        dmix[at] = nt(cz[at], foz[...]).astype(BF16)
+        attend_backward(qkvz.at[at], probz, 2 * h, dmix.at[at], joined.at[at])
         back = norm_backward(
             az[at].astype(F32), cz[at].astype(F32), rstd, gz, joined.at[at], fwz, dn.at[at]
         )
         for j in range(2):
             grads[h, :, j] = back[j * block : (j + 1) * block].reshape(slab * ng, block // (slab * ng), width)
-        gz_begin(3 + h)
+        gz_begin(2 + h)
         gradr[h, :, mine // 2, :, mine % 2] = grads[h, pl.ds(mine * slab, slab)]
 
     kept = []
     for h in range(parts):
         at = pl.ds(h * half, half)
-        gz_end(3 + h)
+        gz_end(2 + h)
         c = gradr[h].reshape(half, width)
         dmix[at] = nt(c, fox[...]).astype(BF16)
-        attend_backward(qkvx.at[at], probs, 2 * h, dmix.at[at], joined.at[at], mask_x, True)
+        attend_backward(qkvx.at[at], probs, 2 * h, dmix.at[at], joined.at[at])
         back = norm_backward(
             ax[at].astype(F32), c.astype(F32), rstd_x[h], gx, joined.at[at], fwx, dn.at[at]
         )
         outs[h] = back.reshape(outs.shape[1:])
-        tr_begin(2 + h)
-        keep = pltpu.make_async_copy(outs.at[h, :, :, me], out.at[:, me, h], local.at[6 + h])
+        tr_begin(1 + h)
+        keep = pltpu.make_async_copy(outs.at[h, :, :, me], out.at[:, me, h], local.at[5 + h])
         keep.start()
         kept.append(keep)
 
@@ -511,15 +635,34 @@
             role1(s, k).wait_send()
             role2(s, k).wait_send()
             role5(s, k).wait_send()
-        role3(k).wait_send()
-        role4(k).wait_send()
+            if over_z(s, k):
+                role3(s, k).wait_send()
+            if two_steps(s, k):
+                role4(s, k).wait_send()
     for h in range(parts):
-        tr_end(2 + h)
+        tr_end(1 + h)
         kept[h].wait()
 
 
-DIRECT = (2, 2, 3, 3)
-TOK_AFTER = 1
+DIRECT = (1, 1, 1, 1)
+TOK_AFTER = 0
+W1_AT = (3, 3, 3, 3)
+COT0, COT1 = 0, 4
+NEAR, WIDE = False, 0
+RELAY1 = (0, 1)
+
+
+def settle(given, out, held, came, went):
+    count = given.shape[0]
+    ins = [pltpu.make_async_copy(given.at[i], held.at[i], came.at[i]) for i in range(count)]
+    outs = [pltpu.make_async_copy(held.at[i], out.at[i], went.at[i]) for i in range(count)]
+    for copy in ins:
+        copy.start()
+    for a, b in zip(ins, outs):
+        a.wait()
+        b.start()
+    for copy in outs:
+        copy.wait()
 
 
 def fits_kernel(trs, gzs, slab, y, x_own, width, depth):
@@ -544,7 +687,6 @@
         out_specs=hbm,
         scratch_shapes=[
             pltpu.VMEM((slab, parts, group, trs, x_own, width), BF16),
-            pltpu.VMEM((slab, parts, group, 2, trs // 2, x_own, width), BF16),
             pltpu.VMEM((z, parts, 2, x_own, width), BF16),
             pltpu.VMEM((parts, *lines), BF16),
             pltpu.VMEM((parts, z, 2, x_own, width), BF16),
@@ -554,17 +696,20 @@
         ]
         + [pltpu.VMEM((width, wide), BF16), pltpu.VMEM((width, width), BF16)] * 2
         + [pltpu.VMEM((rows, wide), BF16)] * 2
-        + [pltpu.VMEM((4 * H, block, block), F32)]
+        + [pltpu.VMEM((4 * H, block, block), F32)] * 2
         + [pltpu.VMEM((rows, width), BF16)] * 2
         + [pltpu.VMEM((rows, wide), BF16), pltpu.VMEM((rows, width), F32)]
         + [pltpu.VMEM((rows, width), BF16)] * 3
         + [
-            pltpu.SemaphoreType.DMA((4, trs)),
-            pltpu.SemaphoreType.DMA((4, trs)),
-            pltpu.SemaphoreType.DMA((5, gzs)),
-            pltpu.SemaphoreType.DMA((5, gzs)),
+            pltpu.SemaphoreType.DMA((3, trs)),
+            pltpu.SemaphoreType.DMA((3, trs)),
+            pltpu.SemaphoreType.DMA((4, gzs)),
+            pltpu.SemaphoreType.DMA((4, gzs)),
             pltpu.SemaphoreType.DMA((2, 4, 6)),
             pltpu.SemaphoreType.DMA((2, 4, 6)),
+            pltpu.SemaphoreType.DMA((4, gzs // 2)),
+            pltpu.SemaphoreType.DMA((4, gzs // 2, 2)),
+            pltpu.SemaphoreType.REGULAR((4,)),
             pltpu.SemaphoreType.DMA((8,)),
         ],
         compiler_params=pltpu.CompilerParams(
@@ -574,7 +719,17 @@
         tokens.reshape(split), cotangent.reshape(split),
         gain_x, wqkv_x, wo_x, gain_z, wqkv_z, wo_z,
     )
-    return result.reshape(tokens.shape)
+    return pl.pallas_call(
+        settle,
+        out_shape=jax.ShapeDtypeStruct(tokens.shape, BF16),
+        in_specs=[hbm],
+        out_specs=hbm,
+        scratch_shapes=[
+            pltpu.VMEM(tokens.shape, BF16),
+            pltpu.SemaphoreType.DMA((slab,)),
+            pltpu.SemaphoreType.DMA((slab,)),
+        ],
+    )(result.reshape(tokens.shape))
 
 
 def solution(mesh):

time: 79 us -> 71.1 us (0.90)
  Pallas kernels: 76.2 us -> 70.9 us
  local copies, waits for them, and re-layouts: 2.15 us -> 0 us
    pallas_call x1, Pallas kernels: 76.2 us -> 69.1 us  [fused(): pl.pallas_call(functools.partial(kernel, trs, gzs, x), out_shape=jax.Shap...]
    unnamed x1 -> x0, local copies, waits for them, and re-layouts: 2.15 us -> none
    pallas_call x0 -> x1, Pallas kernels: none -> 1.81 us  [fused(): pl.pallas_call(settle, out_shape=jax.ShapeDtypeStruct(tokens.shape, BF16)...]
where the time goes in v2:
time: 71.1 us; the launch traced here: 70.9 us
  Pallas kernels  70.9 us (100%)
    pallas_call x1, Pallas kernels, fused(): pl.pallas_call(functools.partial(kernel, trs, gzs, x), out_shape=jax.Shap...  69.1 us
    pallas_call x1, Pallas kernels, fused(): pl.pallas_call(settle, out_shape=jax.ShapeDtypeStruct(tokens.shape, BF16)...  1.81 us

profile of v2, /device:TPU:0, one launch (start us, length us, event | category | flops | bytes accessed | tf_op | source)
XLA Modules:
  0.0 70.9 jit_solution(12136694689967538892)
XLA Ops:
  0.0 69.1 %shard_map.82 = bf16[5,4,2,4,2,768]{5,4,3,2,1,0:T(2,128)(2,1)} custom-call(bf16[5,4,2,4,2,768]{5,4,3,2,1,0:T(2,128)(2,1)} %bitcast.4, bf16[5,4,2,4,2,768]{5,4,3,2,1,0:T(2,128)(2,1)} %bitcast.5, f32[768]{0:T(1024)} %gain_x.1, bf16[192,2304]{1,0:T(8,128)(2,1)} %wx.1, bf16[192,768]{1,0:T(8,128)(2,1)} %ox.1, f32[768]{0:T(1024)} %gain_z.1, bf16[192,2304]{1,0:T(8,128)(2,1)} %wz.1, ...), custom_call_target="tpu_custom_call" | custom-call | tf_op jit(solution)/shard_map/pallas_call | solution.py:683
  69.1 1.8 %shard_map.83 = bf16[5,32,2,768]{3,2,1,0:T(2,128)(2,1)} custom-call(bf16[5,32,2,768]{3,2,1,0:T(2,128)(2,1)} %bitcast.3), custom_call_target="tpu_custom_call" | custom-call | tf_op jit(solution)/shard_map/pallas_call | solution.py:722

commit v3 on v2

--- a/solution.py
+++ b/solution.py
@@ -230,11 +230,12 @@
             joined[at, sp[2]] = dv.astype(BF16)
 
 
-def norm_backward(a, c, rstd, gain, joined, w, dn):
+def norm_backward(a, c, rstd, gain, joined, w, dn, turned):
     width = a.shape[-1]
     part = width // 3
     for j in range(3):
-        dn[:, j * part : (j + 1) * part] = nt(joined[...], w[j * part : (j + 1) * part, :])
+        cols = slice(j * part, (j + 1) * part)
+        dn[:, cols] = nn(joined[...], w[:, cols]) if turned else nt(joined[...], w[cols, :])
     scaled = dn[...] * gain
     mean = jnp.mean(scaled * a, axis=-1, keepdims=True)
     return (c + rstd * (scaled - a * (rstd * rstd) * mean)).astype(BF16)
@@ -244,7 +245,7 @@
     nt_, ng, line_x,
     tok, cot, gain_x, wx, ox, gain_z, wz, oz, out,
     tokr, cotz, mids, midr, grads, gradr, outs,
-    fwx, fox, fwz, foz, qkvx, qkvz, probs, probz, mixed, dmix, joined, dn, ax, az, cz,
+    fwx, fox, fwz, foz, wxt, oxt, qkvx, qkvz, probs, probz, mixed, dmix, joined, dn, ax, az, cz,
     tr_send, tr_recv, gz_send, gz_recv, w_send, w_recv, c_send, c_recv, entered, local,
 ):
     me, mine = lax.axis_index("tr"), lax.axis_index("gz")
@@ -397,6 +398,8 @@
             at = spot(s, k, (sib + 2) % nt_, 0, depth)
         push(s, k, role, at, at, sib, mine).wait_recv()
 
+    turns = (mine // (ng // 2), 1 - mine // (ng // 2))
+
     def tr_copy(n, d):
         t = (me + d) % nt_
         src, dst = tr_ends(n, t, me)
@@ -405,7 +408,9 @@
     def tr_ends(n, to, source):
         if n == 0:
             return tok.at[:, to], tokr.at[:, :, :, source]
-        return outs.at[n - 1, :, :, to], out.at[:, source, n - 1]
+        h, j = (n - 1) // 2, turns[(n - 1) % 2]
+        pair = pl.ds(2 * j, 2)
+        return outs.at[h, :, pair, to], out.at[:, source, h, pair]
 
     def gz_ends(n, to, source):
         if n < 2:
@@ -447,40 +452,53 @@
     core, zc, zs = me % 2, mine // 2, ng // 2
     lanes = (me, sib, across, (sib + 2) % nt_)
 
-    def cot_copy(j, dz, only_at=None):
+    def halves(j):
+        return (0,) if j < 2 else range(parts)
+
+    def cot_ends(j, to, z, source, at_x, h):
+        if j < 2:
+            return cot.at[:, to, :, z], cotz.at[pl.ds(source * slab, slab), :, at_x]
+        return cot.at[:, to, h, z], cotz.at[pl.ds(source * slab, slab), h, at_x]
+
+    def cot_copy(j, dz, h):
         z = (zc + dz) % zs
-        src = cot.at[:, lanes[j], :, z]
-        dst = cotz.at[pl.ds(mine * slab, slab), :, me // 2]
-        return remote(src, dst, c_send.at[j, dz], c_recv.at[j, dz, gy], lanes[j], 2 * z + core)
-
-    def unless_self(j, dz, test, act):
+        src, dst = cot_ends(j, lanes[j], z, mine, me // 2, h)
+        return remote(src, dst, c_send.at[j, dz, h], c_recv.at[j, dz, gy, h], lanes[j], 2 * z + core)
+
+    def unless_self(j, dz, act):
         if j == 0 and dz == 0:
-            pl.when(test)(act)
+            pl.when(core != gy)(act)
         else:
             act()
 
-    def cot_begin(js):
+    def cot_begin(js, h=0):
         for dz in (2, 1, 3, 0):
             for j in js:
-                unless_self(j, dz, core != gy, lambda: cot_copy(j, dz).start())
-
-    def cot_end():
-        for dz in range(zs):
-            for j in range(4):
-                unless_self(j, dz, core != gy, lambda: cot_copy(j, dz).wait_send())
+                unless_self(j, dz, lambda: cot_copy(j, dz, h).start())
+
+    def cot_end(h):
         other = (core + gy) % 2
         for i in range(2):
+            if i == 0 and h > 0:
+                continue
             at_x = (me // 2 + i) % 2
             for dz in range(zs):
                 for ys in range(2):
                     g = 2 * ((zc + zs - dz) % zs) + ys
-                    at = cotz.at[pl.ds(g * slab, slab), :, at_x]
-                    copy = remote(at, at, c_send.at[0, 0], c_recv.at[other + 2 * i, dz, ys], sib, mine)
+                    at = cot_ends(2 * i, me, zc, g, at_x, h)[1]
+                    copy = remote(at, at, c_send.at[0, 0, 0], c_recv.at[other + 2 * i, dz, ys, h], sib, mine)
                     if i == 0 and dz == 0:
                         pl.when((core != gy) | (gy != ys))(lambda: copy.wait_recv())
                     else:
                         copy.wait_recv()
-        pl.when(core == gy)(lambda: cot_self().wait())
+        if h == 0:
+            pl.when(core == gy)(lambda: cot_self().wait())
+
+    def cot_sent():
+        for dz in range(zs):
+            for j in range(4):
+                for h in halves(j):
+                    unless_self(j, dz, lambda: cot_copy(j, dz, h).wait_send())
 
     def cot_self():
         return pltpu.make_async_copy(cot.at[:, me, :, zc], cotz.at[pl.ds(mine * slab, slab), :, me // 2], local.at[7])
@@ -528,6 +546,8 @@
     begin_w1([j for j in ks if W1_AT[j] == 4])
     if COT1 == 4:
         cot_begin((2, 3))
+        if COT2 < 0:
+            cot_begin((2, 3), 1)
     for k in ks:
         arrived(0, k, 4)
         role5(0, k).start()
@@ -540,7 +560,8 @@
     for k in ks:
         role1(1, k).start()
     for h in range(parts):
-        ax[pl.ds(h * half, half)] = tokr[:, h].reshape(half, width)
+        for j in range(2):
+            ax[pl.ds(h * half + j * block, block)] = tokr[:, h, 2 * j : 2 * j + 2].reshape(block, width)
     for k in ks:
         arrived(0, k, 1)
         arrived(0, k, 5)
@@ -555,20 +576,31 @@
     mask_x = line_mask(block, line_x, False)
     mask_z = line_mask(block, block // (slab * ng), True)
     gx, gz = gain_x[...][None], gain_z[...][None]
-    rstd_x = []
     for h in range(parts):
         at = pl.ds(h * half, half)
         a = ax[at].astype(F32)
-        rstd_x.append(rms(a))
-        project(a, rstd_x[h], gx, fwx, qkvx.at[at])
+        project(a, rms(a), gx, fwx, qkvx.at[at])
         attend_forward(qkvx.at[at], probs, 2 * h, mixed.at[at], mask_x)
         mid = ax[at].astype(F32) + nn(mixed[at], fox[...])
-        mids[h] = mid.astype(BF16).reshape(mids.shape[1:])
+        mid = mid.astype(BF16)
+        for j in range(2):
+            spots = mids.at[h, :, 2 * j : 2 * j + 2]
+            spots[...] = mid[j * block : (j + 1) * block].reshape(spots.shape)
         gz_begin(h)
         midr[h, pl.ds(mine * slab, slab)] = mids[h, :, mine // 2, :, mine % 2]
+        if h == COT2:
+            cot_begin((2, 3), 1)
         if h == 0:
             relay_z(RELAY1)
+    def turn(pieces):
+        for k in pieces:
+            at = pl.ds((k % 3) * width, width)
+            turned = (oxt if k == 3 else wxt).at[at]
+            turned[...] = full_w[0][k][:, (k % 3) * width : (k % 3 + 1) * width].T
+
+    turn(T0)
     relay_z([k for k in ks if k not in RELAY1])
+    turn(T1)
     for k in ks:
         arrived(1, k, 2)
         if over_z(1, k):
@@ -599,35 +631,48 @@
     for h in range(parts):
         at = pl.ds(h * half, half)
         rstd = z_front(h)
-        if h == 0:
-            cot_end()
+        cot_end(h)
         for j in range(2):
             cz[pl.ds(h * half + j * block, block)] = cotz[:, h, j].reshape(block, width)
         dmix[at] = nt(cz[at], foz[...]).astype(BF16)
         attend_backward(qkvz.at[at], probz, 2 * h, dmix.at[at], joined.at[at])
         back = norm_backward(
-            az[at].astype(F32), cz[at].astype(F32), rstd, gz, joined.at[at], fwz, dn.at[at]
+            az[at].astype(F32), cz[at].astype(F32), rstd, gz, joined.at[at], fwz, dn.at[at], False
         )
         for j in range(2):
             grads[h, :, j] = back[j * block : (j + 1) * block].reshape(slab * ng, block // (slab * ng), width)
         gz_begin(2 + h)
         gradr[h, :, mine // 2, :, mine % 2] = grads[h, pl.ds(mine * slab, slab)]
 
+    def grads_here(n, j, near):
+        count = ng // 2
+        for d in range(1 if near else 0, count):
+            g = j * count + ((mine + d) % count if near else d)
+            at = gz_ends(n, mine, g)[1]
+            remote(at, at, gz_send.at[n, 0], gz_recv.at[n, (mine + ng - g) % ng], me, g).wait_recv()
+
+    turn(T2)
     kept = []
     for h in range(parts):
-        at = pl.ds(h * half, half)
-        gz_end(2 + h)
-        c = gradr[h].reshape(half, width)
-        dmix[at] = nt(c, fox[...]).astype(BF16)
-        attend_backward(qkvx.at[at], probs, 2 * h, dmix.at[at], joined.at[at])
-        back = norm_backward(
-            ax[at].astype(F32), c.astype(F32), rstd_x[h], gx, joined.at[at], fwx, dn.at[at]
-        )
-        outs[h] = back.reshape(outs.shape[1:])
-        tr_begin(1 + h)
-        keep = pltpu.make_async_copy(outs.at[h, :, :, me], out.at[:, me, h], local.at[5 + h])
-        keep.start()
-        kept.append(keep)
+        for i, j in enumerate(turns):
+            at = pl.ds(pl.multiple_of(h * half + j * block, 16), block)
+            pair = pl.ds(2 * j, 2)
+            a = ax[at].astype(F32)
+            rstd = rms(a)
+            grads_here(2 + h, j, i == 0)
+            c = gradr[h, :, pair].reshape(block, width)
+            dmix[at] = nn(c, oxt[...]).astype(BF16)
+            attend_backward(qkvx.at[at], probs, 2 * h + j, dmix.at[at], joined.at[at])
+            back = norm_backward(
+                ax[at].astype(F32), c.astype(F32), rstd, gx, joined.at[at], wxt, dn.at[at], True
+            )
+            spots = outs.at[h, :, pair]
+            spots[...] = back.reshape(spots.shape)
+            n = 1 + 2 * h + i
+            tr_begin(n)
+            keep = pltpu.make_async_copy(*tr_ends(n, me, me), local.at[7 + n])
+            keep.start()
+            kept.append(keep)
 
     for k in ks:
         for s in range(2):
@@ -639,9 +684,13 @@
                 role3(s, k).wait_send()
             if two_steps(s, k):
                 role4(s, k).wait_send()
+    cot_sent()
     for h in range(parts):
-        tr_end(1 + h)
-        kept[h].wait()
+        for d in range(1, ng):
+            gz_copy(2 + h, d).wait_send()
+    for n, keep in enumerate(kept):
+        tr_end(1 + n)
+        keep.wait()
 
 
 DIRECT = (1, 1, 1, 1)
@@ -649,7 +698,11 @@
 W1_AT = (3, 3, 3, 3)
 COT0, COT1 = 0, 4
 NEAR, WIDE = False, 0
-RELAY1 = (0, 1)
+RELAY1 = (0, 1, 2, 3)
+COT2 = -1
+T0, T1 = (0, 1), (2, 3)
+T2 = ()
+VM = 56
 
 
 def settle(given, out, held, came, went):
@@ -695,25 +748,26 @@
             pltpu.VMEM((parts, slab, group, trs, x_own, width), BF16),
         ]
         + [pltpu.VMEM((width, wide), BF16), pltpu.VMEM((width, width), BF16)] * 2
+        + [pltpu.VMEM((wide, width), BF16), pltpu.VMEM((width, width), BF16)]
         + [pltpu.VMEM((rows, wide), BF16)] * 2
         + [pltpu.VMEM((4 * H, block, block), F32)] * 2
         + [pltpu.VMEM((rows, width), BF16)] * 2
         + [pltpu.VMEM((rows, wide), BF16), pltpu.VMEM((rows, width), F32)]
         + [pltpu.VMEM((rows, width), BF16)] * 3
         + [
-            pltpu.SemaphoreType.DMA((3, trs)),
-            pltpu.SemaphoreType.DMA((3, trs)),
+            pltpu.SemaphoreType.DMA((5, trs)),
+            pltpu.SemaphoreType.DMA((5, trs)),
             pltpu.SemaphoreType.DMA((4, gzs)),
             pltpu.SemaphoreType.DMA((4, gzs)),
             pltpu.SemaphoreType.DMA((2, 4, 6)),
             pltpu.SemaphoreType.DMA((2, 4, 6)),
-            pltpu.SemaphoreType.DMA((4, gzs // 2)),
             pltpu.SemaphoreType.DMA((4, gzs // 2, 2)),
+            pltpu.SemaphoreType.DMA((4, gzs // 2, 2, 2)),
             pltpu.SemaphoreType.REGULAR((4,)),
-            pltpu.SemaphoreType.DMA((8,)),
+            pltpu.SemaphoreType.DMA((12,)),
         ],
         compiler_params=pltpu.CompilerParams(
-            collective_id=0, has_side_effects=True, vmem_limit_bytes=56 * 1024 * 1024
+            collective_id=0, has_side_effects=True, vmem_limit_bytes=VM * 1024 * 1024
         ),
     )(
         tokens.reshape(split), cotangent.reshape(split),

time: 71.1 us -> 67.4 us (0.948)
  Pallas kernels: 70.9 us -> 67.1 us
    pallas_call x1, Pallas kernels: 69.1 us -> 65.3 us  [fused(): pl.pallas_call(functools.partial(kernel, trs, gzs, x), out_shape=jax.Shap...]
where the time goes in v3:
time: 67.4 us; the launch traced here: 67.2 us
  Pallas kernels  67.1 us (100%)
    pallas_call x1, Pallas kernels, fused(): pl.pallas_call(functools.partial(kernel, trs, gzs, x), out_shape=jax.Shap...  65.3 us
    pallas_call x1, Pallas kernels, fused(): pl.pallas_call(settle, out_shape=jax.ShapeDtypeStruct(tokens.shape, BF16)...  1.81 us

profile of v3, /device:TPU:0, one launch (start us, length us, event | category | flops | bytes accessed | tf_op | source)
XLA Modules:
  0.0 67.2 jit_solution(16041087247185162324)
XLA Ops:
  0.0 65.3 %shard_map.82 = bf16[5,4,2,4,2,768]{5,4,3,2,1,0:T(2,128)(2,1)} custom-call(bf16[5,4,2,4,2,768]{5,4,3,2,1,0:T(2,128)(2,1)} %bitcast.4, bf16[5,4,2,4,2,768]{5,4,3,2,1,0:T(2,128)(2,1)} %bitcast.5, f32[768]{0:T(1024)} %gain_x.1, bf16[192,2304]{1,0:T(8,128)(2,1)} %wx.1, bf16[192,768]{1,0:T(8,128)(2,1)} %ox.1, f32[768]{0:T(1024)} %gain_z.1, bf16[192,2304]{1,0:T(8,128)(2,1)} %wz.1, ...), custom_call_target="tpu_custom_call" | custom-call | tf_op jit(solution)/shard_map/pallas_call | solution.py:736
  65.3 1.8 %shard_map.83 = bf16[5,32,2,768]{3,2,1,0:T(2,128)(2,1)} custom-call(bf16[5,32,2,768]{3,2,1,0:T(2,128)(2,1)} %bitcast.3), custom_call_target="tpu_custom_call" | custom-call | tf_op jit(solution)/shard_map/pallas_call | solution.py:776

commit v4 on v3

--- a/solution.py
+++ b/solution.py
@@ -696,10 +696,10 @@
 DIRECT = (1, 1, 1, 1)
 TOK_AFTER = 0
 W1_AT = (3, 3, 3, 3)
-COT0, COT1 = 0, 4
+COT0, COT1 = 0, 5
 NEAR, WIDE = False, 0
 RELAY1 = (0, 1, 2, 3)
-COT2 = -1
+COT2 = 1
 T0, T1 = (0, 1), (2, 3)
 T2 = ()
 VM = 56

time: 67.4 us -> 66.4 us (0.985)
  Pallas kernels: 67.1 us -> 66 us
    pallas_call x1, Pallas kernels: 65.3 us -> 64.2 us  [fused(): pl.pallas_call(functools.partial(kernel, trs, gzs, x), out_shape=jax.Shap...]
where the time goes in v4:
time: 66.4 us; the launch traced here: 66.2 us
  Pallas kernels  66 us (99%)
    pallas_call x1, Pallas kernels, fused(): pl.pallas_call(functools.partial(kernel, trs, gzs, x), out_shape=jax.Shap...  64.2 us
    pallas_call x1, Pallas kernels, fused(): pl.pallas_call(settle, out_shape=jax.ShapeDtypeStruct(tokens.shape, BF16)...  1.81 us

profile of v4, /device:TPU:0, one launch (start us, length us, event | category | flops | bytes accessed | tf_op | source)
XLA Modules:
  0.0 66.2 jit_solution(4864131365489548387)
XLA Ops:
  0.0 64.2 %shard_map.82 = bf16[5,4,2,4,2,768]{5,4,3,2,1,0:T(2,128)(2,1)} custom-call(bf16[5,4,2,4,2,768]{5,4,3,2,1,0:T(2,128)(2,1)} %bitcast.4, bf16[5,4,2,4,2,768]{5,4,3,2,1,0:T(2,128)(2,1)} %bitcast.5, f32[768]{0:T(1024)} %gain_x.1, bf16[192,2304]{1,0:T(8,128)(2,1)} %wx.1, bf16[192,768]{1,0:T(8,128)(2,1)} %ox.1, f32[768]{0:T(1024)} %gain_z.1, bf16[192,2304]{1,0:T(8,128)(2,1)} %wz.1, ...), custom_call_target="tpu_custom_call" | custom-call | tf_op jit(solution)/shard_map/pallas_call | solution.py:736
  64.2 1.8 %shard_map.83 = bf16[5,32,2,768]{3,2,1,0:T(2,128)(2,1)} custom-call(bf16[5,32,2,768]{3,2,1,0:T(2,128)(2,1)} %bitcast.3), custom_call_target="tpu_custom_call" | custom-call | tf_op jit(solution)/shard_map/pallas_call | solution.py:776

commit v5 on v4

--- a/solution.py
+++ b/solution.py
@@ -154,10 +154,12 @@
     return lax.rsqrt(jnp.mean(a * a, axis=-1, keepdims=True) + 1e-06)
 
 
-def project(a, rstd, gain, w, qkv):
+def project(a, rstd, gain, w, qkv, before=None):
     width = a.shape[1]
     normed = (a * rstd * gain).astype(BF16)
     for j in range(3):
+        if before is not None:
+            before(j)
         cols = slice(j * width, (j + 1) * width)
         qkv[:, cols] = nn(normed, w[:, cols]).astype(BF16)
 
@@ -613,9 +615,11 @@
         if two_steps(1, k):
             arrived(1, k, 4)
             role5(1, k).start()
-    for k in ks:
+
+    def whole_z(k):
         arrived(1, k, 1)
         arrived(1, k, 5)
+
 
     def z_front(h):
         at = pl.ds(h * half, half)
@@ -624,13 +628,15 @@
             az[pl.ds(h * half + j * block, block)] = midr[h, :, j].reshape(block, width)
         a = az[at].astype(F32)
         rstd = rms(a)
-        project(a, rstd, gz, fwz, qkvz.at[at])
+        project(a, rstd, gz, fwz, qkvz.at[at], whole_z if h == 0 else None)
         attend_scores(qkvz.at[at], probz, 2 * h, mask_z)
         return rstd
 
     for h in range(parts):
         at = pl.ds(h * half, half)
         rstd = z_front(h)
+        if h == 0:
+            whole_z(3)
         cot_end(h)
         for j in range(2):
             cz[pl.ds(h * half + j * block, block)] = cotz[:, h, j].reshape(block, width)

time: 66.4 us -> 65.5 us (0.986)
  Pallas kernels: 66 us -> 65 us
    pallas_call x1, Pallas kernels: 64.2 us -> 63.2 us  [fused(): pl.pallas_call(functools.partial(kernel, trs, gzs, x), out_shape=jax.Shap...]
where the time goes in v5:
time: 65.5 us; the launch traced here: 65.1 us
  Pallas kernels  65 us (99%)
    pallas_call x1, Pallas kernels, fused(): pl.pallas_call(functools.partial(kernel, trs, gzs, x), out_shape=jax.Shap...  63.2 us
    pallas_call x1, Pallas kernels, fused(): pl.pallas_call(settle, out_shape=jax.ShapeDtypeStruct(tokens.shape, BF16)...  1.81 us

profile of v5, /device:TPU:0, one launch (start us, length us, event | category | flops | bytes accessed | tf_op | source)
XLA Modules:
  0.0 65.1 jit_solution(5781531095345335784)
XLA Ops:
  0.0 63.2 %shard_map.82 = bf16[5,4,2,4,2,768]{5,4,3,2,1,0:T(2,128)(2,1)} custom-call(bf16[5,4,2,4,2,768]{5,4,3,2,1,0:T(2,128)(2,1)} %bitcast.4, bf16[5,4,2,4,2,768]{5,4,3,2,1,0:T(2,128)(2,1)} %bitcast.5, f32[768]{0:T(1024)} %gain_x.1, bf16[192,2304]{1,0:T(8,128)(2,1)} %wx.1, bf16[192,768]{1,0:T(8,128)(2,1)} %ox.1, f32[768]{0:T(1024)} %gain_z.1, bf16[192,2304]{1,0:T(8,128)(2,1)} %wz.1, ...), custom_call_target="tpu_custom_call" | custom-call | tf_op jit(solution)/shard_map/pallas_call | solution.py:742
  63.2 1.8 %shard_map.83 = bf16[5,32,2,768]{3,2,1,0:T(2,128)(2,1)} custom-call(bf16[5,32,2,768]{3,2,1,0:T(2,128)(2,1)} %bitcast.3), custom_call_target="tpu_custom_call" | custom-call | tf_op jit(solution)/shard_map/pallas_call | solution.py:782
